TPU v7x, 32 devices: a whole 2x2x4 slice. The times are simulated.
32 devices in a mesh: fsdp: 8 (over y, x, core), tp: 4 (over z).
Axes of the slice: x: 2, y: 2, z: 4, core: 2. Of those that a mesh axis runs over, the one named last changes fastest.
Arguments:
- inputs: bfloat16 [8192, 768], P(('fsdp', 'tp')), may hold values from -6 to 6
- cotangent: bfloat16 [8192, 768], P(('fsdp', 'tp')), may hold values from -6 to 6
- qkv_weight: bfloat16 [2, 3, 768, 768], P(None, None, 'fsdp', 'tp'), may hold values from -0.21875 to 0.21875
- out_weight: bfloat16 [2, 768, 768], P(None, 'tp', 'fsdp'), may hold values from -0.875 to 0.875
- attn_gain: bfloat16 [2, 768], P(None, 'fsdp'), may hold values from 0.25 to 1.75
- ffn_gain: bfloat16 [2, 768], P(None, 'fsdp'), may hold values from 0.25 to 1.75
- router_weight: bfloat16 [2, 768, 4], P(None, 'fsdp'), may hold values from -0.15625 to 0.15625
- in_weight: bfloat16 [2, 4, 768, 3072], P(None, None, 'fsdp', 'tp'), may hold values from -0.21875 to 0.21875
- down_weight: bfloat16 [2, 4, 3072, 768], P(None, None, 'tp', 'fsdp'), may hold values from -0.4375 to 0.4375
- routes: int32 [8192], P('fsdp'), may hold values from 0 to 3, as said below
- slots: int32 [8192], P('fsdp'), may hold values from 0 to 256, as said below
Outputs:
- outputs: float32 [8192, 768], P(('fsdp', 'tp'))
- d_inputs: float32 [8192, 768], P(('fsdp', 'tp'))
- d_qkv_weight: float32 [2, 3, 768, 768], P(None, None, 'fsdp', 'tp')
- d_out_weight: float32 [2, 768, 768], P(None, 'tp', 'fsdp')
- d_attn_gain: float32 [2, 768], P(None, 'fsdp')
- d_ffn_gain: float32 [2, 768], P(None, 'fsdp')
- d_router_weight: float32 [2, 768, 4], P(None, 'fsdp')
- d_in_weight: float32 [2, 4, 768, 3072], P(None, None, 'fsdp', 'tp')
- d_down_weight: float32 [2, 4, 3072, 768], P(None, None, 'tp', 'fsdp')
Inputs may be any that keep to these rules, and one draw needn't show every extreme that they name: `routes`: the expert of a token; in each group one expert drawn from the seed is named by more than 256 tokens. A token's rank, in order of position, among the tokens of its group with the same route, with ranks of 256 or more given as 256 (the token is dropped); in every group some expert fills all 256 slots and drops tokens.
All inputs are finite; a program needn't handle non-finite values.
Results may differ from a plain program's by a relative error of at most 0.028.
Values may be sent and summed in bfloat16 or wider, within the bound.
A program may use at most 192 MiB of HBM per device.

v0:
```python
import jax
import jax.numpy as jnp
from jax import lax
from jax.sharding import PartitionSpec as P

DH = 64
LAYERS = 2
SEQ = 1024
SEQS = 1


EPSILON = 1e-06
HIGH = lax.Precision.HIGHEST


def normed(hidden, gain_row):
    scale_inv = lax.rsqrt(jnp.mean(hidden * hidden, -1, keepdims=True) + EPSILON)
    return hidden * scale_inv * gain_row


def normed_back(hidden, gain_row, upstream):
    _, pull_back = jax.vjp(normed, hidden, gain_row)
    return pull_back(upstream)


def gelu_back(before, upstream):
    _, pull_back = jax.vjp(jax.nn.gelu, before)
    return pull_back(upstream)[0]


def slot_tables(route_part, slot_part, experts, capacity):
    is_live = slot_part < capacity
    position = jnp.where(is_live, route_part * capacity + slot_part, experts * capacity)
    row_total = route_part.shape[0]
    token_of = (
        jnp.zeros((experts * capacity + 1,), jnp.int32)
        .at[position]
        .set(jnp.arange(row_total, dtype=jnp.int32))[:-1]
    )
    filled = jnp.zeros((experts * capacity + 1,), jnp.bool_).at[position].set(True)[:-1]
    return (is_live, jnp.where(is_live, position, 0), token_of, filled)


def attend_ahead(triple):
    query, key_rows, value_rows = triple
    scale = query.shape[-1] ** (-0.5)
    scores = jnp.einsum("qhd,khd->hqk", query, key_rows, preferred_element_type=jnp.float32) * scale
    top_score = jnp.max(scores, -1, keepdims=True)
    expon = jnp.exp(scores - top_score)
    totals = jnp.sum(expon, -1, keepdims=True)
    rounded = (expon / totals).astype(jnp.bfloat16)
    mixed = jnp.einsum("hqk,khd->qhd", rounded, value_rows, preferred_element_type=jnp.float32)
    return (mixed.astype(jnp.bfloat16), top_score + jnp.log(totals))


def attend_behind(items):
    query, key_rows, value_rows, log_total, d_mixed = items
    scale = query.shape[-1] ** (-0.5)
    scores = jnp.einsum("qhd,khd->hqk", query, key_rows, preferred_element_type=jnp.float32) * scale
    probs = jnp.exp(scores - log_total)
    rounded = probs.astype(jnp.bfloat16)
    d_probs = jnp.einsum("qhd,khd->hqk", d_mixed, value_rows, preferred_element_type=jnp.float32)
    d_scores = probs * (d_probs - jnp.sum(probs * d_probs, -1, keepdims=True))
    d_scaled = (d_scores * scale).astype(jnp.bfloat16)
    d_query = jnp.einsum(
        "hqk,khd->qhd", d_scaled, key_rows, preferred_element_type=jnp.float32
    ).astype(jnp.bfloat16)
    d_key = jnp.einsum("hqk,qhd->khd", d_scaled, query, preferred_element_type=jnp.float32).astype(
        jnp.bfloat16
    )
    d_value = jnp.einsum(
        "hqk,qhd->khd", rounded, d_mixed, preferred_element_type=jnp.float32
    ).astype(jnp.bfloat16)
    return (d_query, d_key, d_value)


def local(
    inputs,
    cotangent,
    qkv_weight,
    out_weight,
    attn_gain,
    ffn_gain,
    router_weight,
    in_weight,
    down_weight,
    routes,
    slots,
):
    tp_index = lax.axis_index("tp")
    tok_here = inputs.shape[0]
    experts = in_weight.shape[1]
    group_tok = routes.shape[0]
    capacity = group_tok // experts
    is_live, position, token_of, filled = slot_tables(routes, slots, experts, capacity)
    route_here = lax.dynamic_slice_in_dim(routes, tp_index * tok_here, tok_here)
    pick = (route_here[:, None] == jnp.arange(experts, dtype=jnp.int32)[None, :]).astype(
        jnp.float32
    )
    hidden = inputs.astype(jnp.float32)
    saved = []
    for layer_index in range(LAYERS):
        full_set = (
            lax.all_gather(qkv_weight[layer_index], "fsdp", axis=1, tiled=True),
            lax.all_gather(out_weight[layer_index], "fsdp", axis=1, tiled=True),
            lax.all_gather(attn_gain[layer_index], "fsdp", axis=0, tiled=True),
            lax.all_gather(ffn_gain[layer_index], "fsdp", axis=0, tiled=True),
            lax.all_gather(router_weight[layer_index], "fsdp", axis=0, tiled=True),
            lax.all_gather(in_weight[layer_index], "fsdp", axis=1, tiled=True),
            lax.all_gather(down_weight[layer_index], "fsdp", axis=2, tiled=True),
        )
        wqkv, wout, gain_one, gain_two, router_full, win, wdown = full_set
        heads_here = wqkv.shape[2] // DH
        a_here = normed(hidden, gain_one.astype(jnp.float32)).astype(jnp.bfloat16)
        a_rows = lax.all_gather(a_here, "tp", axis=0, tiled=True)
        qkv = jnp.einsum("td,cdf->ctf", a_rows, wqkv, preferred_element_type=jnp.float32).astype(
            jnp.bfloat16
        )
        shaped = qkv.reshape(3, SEQS, SEQ, heads_here, DH)
        mixed, log_total = lax.map(attend_ahead, (shaped[0], shaped[1], shaped[2]))
        mixed = mixed.reshape(group_tok, heads_here * DH)
        partial_attn = jnp.dot(mixed, wout, preferred_element_type=jnp.float32)
        middle = hidden + lax.psum_scatter(
            partial_attn.astype(jnp.bfloat16), "tp", scatter_dimension=0, tiled=True
        ).astype(jnp.float32)
        b_here = normed(middle, gain_two.astype(jnp.float32)).astype(jnp.bfloat16)
        logits = jnp.dot(b_here, router_full, preferred_element_type=jnp.float32)
        probs = jax.nn.softmax(logits, -1)
        gate = jnp.sum(probs * pick, -1)
        b_rows = lax.all_gather(b_here, "tp", axis=0, tiled=True)
        buffer = jnp.where(filled[:, None], b_rows[token_of], jnp.zeros((), jnp.bfloat16)).reshape(
            experts, capacity, b_rows.shape[1]
        )
        pre = jnp.einsum("ecd,edf->ecf", buffer, win, preferred_element_type=jnp.float32)
        act = jax.nn.gelu(pre).astype(jnp.bfloat16)
        expert_out = jnp.einsum(
            "ecf,efd->ecd", act, wdown, preferred_element_type=jnp.float32
        ).reshape(experts * capacity, -1)
        token_out = jnp.where(is_live[:, None], expert_out[position], 0.0)
        combined = lax.psum_scatter(
            token_out.astype(jnp.bfloat16), "tp", scatter_dimension=0, tiled=True
        ).astype(jnp.float32)
        saved.append(
            (
                full_set,
                hidden,
                a_rows,
                shaped,
                log_total,
                mixed,
                middle,
                b_here,
                probs,
                gate,
                combined,
                buffer,
                pre,
                act,
            )
        )
        hidden = middle + gate[:, None] * combined
    upstream = cotangent.astype(jnp.float32)
    grad_lists = [[None] * LAYERS for list_index in range(7)]
    for layer_index in reversed(range(LAYERS)):
        (
            kept_set,
            before,
            a_rows,
            shaped,
            log_total,
            mixed,
            middle,
            b_here,
            probs,
            gate,
            combined,
            buffer,
            pre,
            act,
        ) = saved[layer_index]
        full_set = (
            lax.all_gather(qkv_weight[layer_index], "fsdp", axis=1, tiled=True),
            lax.all_gather(out_weight[layer_index], "fsdp", axis=1, tiled=True),
            lax.all_gather(attn_gain[layer_index], "fsdp", axis=0, tiled=True),
            lax.all_gather(ffn_gain[layer_index], "fsdp", axis=0, tiled=True),
            lax.all_gather(router_weight[layer_index], "fsdp", axis=0, tiled=True),
            lax.all_gather(in_weight[layer_index], "fsdp", axis=1, tiled=True),
            lax.all_gather(down_weight[layer_index], "fsdp", axis=2, tiled=True),
        )
        wqkv, wout, gain_one, gain_two, router_full, win, wdown = full_set
        heads_here = wqkv.shape[2] // DH
        d_combined = (gate[:, None] * upstream).astype(jnp.bfloat16)
        d_gate = jnp.sum(upstream * combined, -1)
        d_comb_rows = lax.all_gather(d_combined, "tp", axis=0, tiled=True)
        d_expert_out = jnp.where(
            filled[:, None], d_comb_rows[token_of], jnp.zeros((), jnp.bfloat16)
        ).reshape(experts, capacity, -1)
        d_act = jnp.einsum("ecd,efd->ecf", d_expert_out, wdown, preferred_element_type=jnp.float32)
        grad_down = jnp.einsum(
            "ecf,ecd->def", act, d_expert_out, preferred_element_type=jnp.float32
        )
        d_pre = gelu_back(pre, d_act).astype(jnp.bfloat16)
        grad_in = jnp.einsum("ecd,ecf->def", buffer, d_pre, preferred_element_type=jnp.float32)
        d_buffer = jnp.einsum(
            "ecf,edf->ecd", d_pre, win, preferred_element_type=jnp.float32
        ).reshape(experts * capacity, -1)
        d_tokens = jnp.where(is_live[:, None], d_buffer[position], 0.0)
        d_b_here = lax.psum_scatter(
            d_tokens.astype(jnp.bfloat16), "tp", scatter_dimension=0, tiled=True
        ).astype(jnp.float32)
        d_logits = d_gate[:, None] * gate[:, None] * (pick - probs)
        router_float = router_full.astype(jnp.float32)
        d_b_here = d_b_here + jnp.dot(d_logits, router_float.T, precision=HIGH)
        grad_router = jnp.dot(b_here.astype(jnp.float32).T, d_logits, precision=HIGH)
        d_middle, grad_gain_two = normed_back(middle, gain_two.astype(jnp.float32), d_b_here)
        d_middle = d_middle + upstream
        d_attn_rows = lax.all_gather(d_middle.astype(jnp.bfloat16), "tp", axis=0, tiled=True)
        d_mixed = jnp.einsum(
            "td,fd->tf", d_attn_rows, wout, preferred_element_type=jnp.float32
        ).astype(jnp.bfloat16)
        grad_out = jnp.einsum("tf,td->df", mixed, d_attn_rows, preferred_element_type=jnp.float32)
        d_mixed_shaped = d_mixed.reshape(SEQS, SEQ, heads_here, DH)
        d_query, d_key, d_value = lax.map(
            attend_behind, (shaped[0], shaped[1], shaped[2], log_total, d_mixed_shaped)
        )
        d_qkv = jnp.stack([d_query, d_key, d_value]).reshape(3, group_tok, heads_here * DH)
        grad_qkv = jnp.einsum("td,ctf->dcf", a_rows, d_qkv, preferred_element_type=jnp.float32)
        d_a_rows = jnp.einsum("ctf,cdf->td", d_qkv, wqkv, preferred_element_type=jnp.float32)
        d_a_here = lax.psum_scatter(
            d_a_rows.astype(jnp.bfloat16), "tp", scatter_dimension=0, tiled=True
        ).astype(jnp.float32)
        d_before, grad_gain_one = normed_back(before, gain_one.astype(jnp.float32), d_a_here)
        upstream = d_before + d_middle
        shards = (
            lax.psum_scatter(grad_qkv, "fsdp", scatter_dimension=0, tiled=True),
            lax.psum_scatter(grad_out, "fsdp", scatter_dimension=0, tiled=True),
            lax.psum_scatter(grad_gain_one, "fsdp", scatter_dimension=0, tiled=True),
            lax.psum_scatter(grad_gain_two, "fsdp", scatter_dimension=0, tiled=True),
            lax.psum_scatter(grad_router, "fsdp", scatter_dimension=0, tiled=True),
            lax.psum_scatter(grad_in, "fsdp", scatter_dimension=0, tiled=True),
            lax.psum_scatter(grad_down, "fsdp", scatter_dimension=0, tiled=True),
        )
        shared = lax.psum((shards[2], shards[3], shards[4]), "tp")
        layer_grads = (
            jnp.transpose(shards[0], (1, 0, 2)),
            shards[1].T,
            shared[0],
            shared[1],
            shared[2],
            jnp.transpose(shards[5], (1, 0, 2)),
            jnp.transpose(shards[6], (1, 2, 0)),
        )
        for slot_index in range(7):
            grad_lists[slot_index][layer_index] = layer_grads[slot_index]
    stacked = [jnp.stack(grad_lists[slot_index]) for slot_index in range(7)]
    return (
        hidden,
        upstream,
        stacked[0],
        stacked[1],
        stacked[2],
        stacked[3],
        stacked[4],
        stacked[5],
        stacked[6],
    )


def solution(mesh):
    return jax.shard_map(
        local,
        mesh=mesh,
        in_specs=(
            P(("fsdp", "tp"), None),
            P(("fsdp", "tp"), None),
            P(None, None, "fsdp", "tp"),
            P(None, "tp", "fsdp"),
            P(None, "fsdp"),
            P(None, "fsdp"),
            P(None, "fsdp", None),
            P(None, None, "fsdp", "tp"),
            P(None, None, "tp", "fsdp"),
            P("fsdp"),
            P("fsdp"),
        ),
        out_specs=(
            P(("fsdp", "tp"), None),
            P(("fsdp", "tp"), None),
            P(None, None, "fsdp", "tp"),
            P(None, "tp", "fsdp"),
            P(None, "fsdp"),
            P(None, "fsdp"),
            P(None, "fsdp", None),
            P(None, None, "fsdp", "tp"),
            P(None, None, "tp", "fsdp"),
        ),
        check_vma=False,
    )
```

profile of v0, /device:TPU:0, one launch (start us, length us, event | category | flops | bytes accessed | tf_op | source)
XLA Modules:
  0.0 1629.4 jit_solution(15794501557190111187)
XLA Ops:
  11.6 16.0 all-reduce.13
  33.1 12.3 all-gather.1
  47.1 9.3 all-gather.2
  56.8 11.7 all-gather.27.cloned.1.call-done
  83.1 34.2 %reduce-scatter.21.cloned.1.call-done = bf16[256,768]{1,0:T(8,128)(2,1)} async-done(((bf16[1024,768]{1,0:T(8,128)(2,1)}), bf16[256,768]{1,0:T(8,128)(2,1)}) %reduce-scatter.21.cloned.1.call-update) | async-done | bytes 393232 | tf_op jit(solution)/shard_map/reduce_scatter | solution.py:123
  133.5 23.3 %all-gather.29.cloned.1.call-done = bf16[1024,768]{1,0:T(8,128)(2,1)} async-done(((bf16[256,768]{1,0:T(8,128)(2,1)}), bf16[1024,768]{1,0:T(8,128)(2,1)}) %all-gather.29.cloned.1.call-update) | async-done | bytes 1572880 | tf_op jit(solution)/shard_map/all_gather | solution.py:130
  156.7 7.2 gather_fusion
  165.7 31.2 %all-gather.45.cloned.1.call-done = bf16[1,4,768,768]{2,1,0,3:T(4,128)(2,1)} async-done(((bf16[1,4,768,96]{2,1,0,3:T(4,128)(2,1)}), bf16[1,4,768,768]{2,1,0,3:T(4,128)(2,1)}) %all-gather.45.cloned.1.call-update) | async-done | bytes 4718608 | tf_op jit(solution)/shard_map/all_gather | solution.py:110
  196.9 8.5 copy.96
  205.3 32.8 %all-gather.43.cloned.1.call-done = bf16[1,4,768,768]{3,2,1,0:T(8,128)(2,1)} async-done(((bf16[1,4,96,768]{3,2,1,0:T(8,128)(2,1)}), bf16[1,4,768,768]{3,2,1,0:T(8,128)(2,1)}) %all-gather.43.cloned.1.call-update) | async-done | bytes 4718608 | tf_op jit(solution)/shard_map/all_gather | solution.py:109
  252.8 9.5 all-gather.4
  263.6 23.9 %reduce-scatter.23.cloned.1.call-done = bf16[256,768]{1,0:T(8,128)(2,1)} async-done(((bf16[1024,768]{1,0:T(8,128)(2,1)}), bf16[256,768]{1,0:T(8,128)(2,1)}) %reduce-scatter.23.cloned.1.call-update) | async-done | bytes 393232 | tf_op jit(solution)/shard_map/reduce_scatter | solution.py:140
  290.0 13.5 all-gather.8
  305.6 9.3 all-gather.9
  315.4 10.6 all-gather.31.cloned.1.call-done
  342.3 32.9 %reduce-scatter.25.cloned.1.call-done = bf16[256,768]{1,0:T(8,128)(2,1)} async-done(((bf16[1024,768]{1,0:T(8,128)(2,1)}), bf16[256,768]{1,0:T(8,128)(2,1)}) %reduce-scatter.25.cloned.1.call-update) | async-done | bytes 393232 | tf_op jit(solution)/shard_map/reduce_scatter | solution.py:123
  379.3 36.3 %all-gather.49.cloned.1.call-done = bf16[1,4,768,768]{2,1,0,3:T(4,128)(2,1)} async-done(((bf16[1,4,768,96]{2,1,0,3:T(4,128)(2,1)}), bf16[1,4,768,768]{2,1,0,3:T(4,128)(2,1)}) %all-gather.49.cloned.1.call-update) | async-done | bytes 4718608 | tf_op jit(solution)/shard_map/all_gather | solution.py:110
  415.6 8.5 copy.107
  424.1 30.1 %all-gather.33.cloned.1.call-done = bf16[1024,768]{1,0:T(8,128)(2,1)} async-done(((bf16[256,768]{1,0:T(8,128)(2,1)}), bf16[1024,768]{1,0:T(8,128)(2,1)}) %all-gather.33.cloned.1.call-update) | async-done | bytes 1572880 | tf_op jit(solution)/shard_map/all_gather | solution.py:130
  454.1 7.2 gather_fusion.2
  463.1 31.3 %all-gather.47.cloned.1.call-done = bf16[1,4,768,768]{3,2,1,0:T(8,128)(2,1)} async-done(((bf16[1,4,96,768]{3,2,1,0:T(8,128)(2,1)}), bf16[1,4,768,768]{3,2,1,0:T(8,128)(2,1)}) %all-gather.47.cloned.1.call-update) | async-done | bytes 4718608 | tf_op jit(solution)/shard_map/all_gather | solution.py:109
  511.6 9.5 all-gather.11
  521.8 25.1 %reduce-scatter.27.cloned.1.call-done = bf16[256,768]{1,0:T(8,128)(2,1)} async-done(((bf16[1024,768]{1,0:T(8,128)(2,1)}), bf16[256,768]{1,0:T(8,128)(2,1)}) %reduce-scatter.27.cloned.1.call-update) | async-done | bytes 393232 | tf_op jit(solution)/shard_map/reduce_scatter | solution.py:140
  548.9 36.2 %all-gather.35.cloned.1.call-done = bf16[1024,768]{1,0:T(8,128)(2,1)} async-done(((bf16[256,768]{1,0:T(8,128)(2,1)}), bf16[1024,768]{1,0:T(8,128)(2,1)}) %all-gather.35.cloned.1.call-update) | async-done | bytes 1572880 | tf_op jit(solution)/shard_map/all_gather | solution.py:194
  585.1 7.2 gather_fusion.4
  615.4 33.8 %reduce-scatter.29.cloned.1.call-done = bf16[256,768]{1,0:T(8,128)(2,1)} async-done(((bf16[1024,768]{1,0:T(8,128)(2,1)}), bf16[256,768]{1,0:T(8,128)(2,1)}) %reduce-scatter.29.cloned.1.call-update) | async-done | bytes 393232 | tf_op jit(solution)/shard_map/reduce_scatter | solution.py:208
  654.1 35.5 %all-gather.37.cloned.1.call-done = bf16[1024,768]{1,0:T(8,128)(2,1)} async-done(((bf16[256,768]{1,0:T(8,128)(2,1)}), bf16[1024,768]{1,0:T(8,128)(2,1)}) %all-gather.37.cloned.1.call-update) | async-done | bytes 1572880 | tf_op jit(solution)/shard_map/all_gather | solution.py:217
  705.1 22.8 %fusion.101 = bf16[3,64,1024]{2,1,0:T(8,128)(2,1)} fusion(bf16[1024,3,64]{0,2,1:T(8,128)(2,1)S(1)} %bitcast.237, f32[3,1024,1024]{1,2,0:T(8,128)} %fusion.218, f32[3,1024,1024]{1,2,0:T(8,128)} %copy-done.1, f32[3,1024]{1,0:T(4,128)} %log_add_fusion), kind=kOutput, calls=%fused_computation.120 | convolution fusion | flops 431165440 | bytes 25964544 | tf_op jit(solution)/shard_map/while/body/eval_jaxpr/hqk,qhd->khd/dot_general | solution.py:68
  727.9 22.4 %fusion.98 = bf16[3,64,1024]{2,1,0:T(8,128)(2,1)} fusion(bf16[1024,3,64]{0,2,1:T(8,128)(2,1)S(1)} %bitcast.235, f32[3,1024,1024]{1,2,0:T(8,128)} %fusion.218, f32[3,1024,1024]{1,2,0:T(8,128)} %copy-done.1, f32[3,1024]{1,0:T(4,128)} %log_add_fusion), kind=kOutput, calls=%fused_computation.119 | convolution fusion | flops 431165440 | bytes 25964544 | tf_op jit(solution)/shard_map/while/body/eval_jaxpr/hqk,khd->qhd/dot_general | solution.py:65
  754.5 34.3 %reduce-scatter.31.cloned.1.call-done = bf16[256,768]{1,0:T(8,128)(2,1)} async-done(((bf16[1024,768]{1,0:T(8,128)(2,1)}), bf16[256,768]{1,0:T(8,128)(2,1)}) %reduce-scatter.31.cloned.1.call-update) | async-done | bytes 393232 | tf_op jit(solution)/shard_map/reduce_scatter | solution.py:229
  795.7 36.1 %all-gather.39.cloned.1.call-done = bf16[1024,768]{1,0:T(8,128)(2,1)} async-done(((bf16[256,768]{1,0:T(8,128)(2,1)}), bf16[1024,768]{1,0:T(8,128)(2,1)}) %all-gather.39.cloned.1.call-update) | async-done | bytes 1572880 | tf_op jit(solution)/shard_map/all_gather | solution.py:194
  831.8 7.3 gather_fusion.6
  842.0 7.2 fusion.68
  861.9 34.2 %reduce-scatter.33.cloned.1.call-done = bf16[256,768]{1,0:T(8,128)(2,1)} async-done(((bf16[1024,768]{1,0:T(8,128)(2,1)}), bf16[256,768]{1,0:T(8,128)(2,1)}) %reduce-scatter.33.cloned.1.call-update) | async-done | bytes 393232 | tf_op jit(solution)/shard_map/reduce_scatter | solution.py:208
  907.1 28.8 %all-gather.41.cloned.1.call-done = bf16[1024,768]{1,0:T(8,128)(2,1)} async-done(((bf16[256,768]{1,0:T(8,128)(2,1)}), bf16[1024,768]{1,0:T(8,128)(2,1)}) %all-gather.41.cloned.1.call-update) | async-done | bytes 1572880 | tf_op jit(solution)/shard_map/all_gather | solution.py:217
  952.1 19.4 %fusion.95 = bf16[3,64,1024]{2,1,0:T(8,128)(2,1)S(1)} fusion(bf16[1024,3,64]{0,2,1:T(8,128)(2,1)S(1)} %bitcast.231, f32[3,1024,1024]{1,2,0:T(8,128)} %fusion.219, f32[3,1024,1024]{1,2,0:T(8,128)} %copy-done, f32[3,1024]{1,0:T(4,128)S(1)} %log_add_fusion.1), kind=kOutput, calls=%fused_computation.118 | convolution fusion | flops 431165440 | bytes 25964544 | tf_op jit(solution)/shard_map/while/body/eval_jaxpr/hqk,qhd->khd/dot_general | solution.py:68
  971.5 19.0 %fusion.92 = bf16[3,64,1024]{2,1,0:T(8,128)(2,1)S(1)} fusion(bf16[1024,3,64]{0,2,1:T(8,128)(2,1)S(1)} %bitcast.229, f32[3,1024,1024]{1,2,0:T(8,128)} %fusion.219, f32[3,1024,1024]{1,2,0:T(8,128)} %copy-done, f32[3,1024]{1,0:T(4,128)S(1)} %log_add_fusion.1), kind=kOutput, calls=%fused_computation.117 | convolution fusion | flops 431165440 | bytes 25964544 | tf_op jit(solution)/shard_map/while/body/eval_jaxpr/hqk,khd->qhd/dot_general | solution.py:65
  1012.5 12.3 copy.125
  1031.2 12.1 copy.122
  1062.8 22.0 %reduce-scatter.41.cloned.1.call-done = f32[96,192]{1,0:T(8,128)} async-done(((f32[768,192]{1,0:T(8,128)}), f32[96,192]{1,0:T(8,128)}) %reduce-scatter.41.cloned.1.call-update) | async-done | bytes 73744 | tf_op jit(solution)/shard_map/reduce_scatter | solution.py:236
  1086.6 44.5 %reduce-scatter.39.cloned.1.call-done = f32[96,3,192]{2,0,1:T(8,128)} async-done(((f32[768,3,192]{2,0,1:T(8,128)}), f32[96,3,192]{2,0,1:T(8,128)}) %reduce-scatter.39.cloned.1.call-update) | async-done | bytes 221200 | tf_op jit(solution)/shard_map/reduce_scatter | solution.py:235
  1131.2 46.8 %reduce-scatter.37.cloned.1.call-done = f32[96,3,192]{2,0,1:T(8,128)} async-done(((f32[768,3,192]{2,0,1:T(8,128)}), f32[96,3,192]{2,0,1:T(8,128)}) %reduce-scatter.37.cloned.1.call-update) | async-done | bytes 221200 | tf_op jit(solution)/shard_map/reduce_scatter | solution.py:235
  1179.9 35.6 %reduce-scatter.35.cloned.1.call-done = bf16[256,768]{1,0:T(8,128)(2,1)} async-done(((bf16[1024,768]{1,0:T(8,128)(2,1)}), bf16[256,768]{1,0:T(8,128)(2,1)}) %reduce-scatter.35.cloned.1.call-update) | async-done | bytes 393232 | tf_op jit(solution)/shard_map/reduce_scatter | solution.py:229
  1216.8 24.9 %all-reduce.10 = (f32[768]{0:T(1024)S(1)}, f32[768]{0:T(1024)S(1)}, f32[768]{0:T(1024)S(1)}, f32[768]{0:T(1024)S(1)}) all-reduce(f32[768]{0:T(1024)S(1)} %copy-done.80, f32[768]{0:T(1024)S(1)} %get-tuple-element.132, f32[768]{0:T(1024)S(1)} %copy-done.79, f32[768]{0:T(1024)S(1)} %copy-done.107), channel_id=29, replica_groups=mesh['fsdp'=8,'tp'=4] {'fsdp'}, use_global_device_ids=true, to_apply=%region_40.41.clone | all-reduce | flops 3072 | bytes 24576
  1241.8 9.9 all-reduce.12
  1255.9 202.5 %all-reduce.16.cloned.1.call-done = (f32[768,4,768]{2,1,0:T(4,128)}, f32[768,4,768]{2,1,0:T(4,128)}) async-done(((f32[768,4,768]{2,1,0:T(4,128)}, f32[768,4,768]{2,1,0:T(4,128)}), (f32[768,4,768]{2,1,0:T(4,128)}, f32[768,4,768]{2,1,0:T(4,128)})) %all-reduce.16.cloned.1.call-update) | async-done | bytes 18874384
  1462.8 76.1 %reduce-scatter.47.cloned.1.call-done = f32[96,4,768]{2,0,1:T(8,128)} async-done(((f32[768,4,768]{2,0,1:T(8,128)}), f32[96,4,768]{2,0,1:T(8,128)}) %reduce-scatter.47.cloned.1.call-update) | async-done | bytes 1179664 | tf_op jit(solution)/shard_map/reduce_scatter | solution.py:241
  1538.9 80.4 %reduce-scatter.45.cloned.1.call-done = f32[96,4,768]{2,0,1:T(8,128)} async-done(((f32[768,4,768]{2,0,1:T(8,128)}), f32[96,4,768]{2,0,1:T(8,128)}) %reduce-scatter.45.cloned.1.call-update) | async-done | bytes 1179664 | tf_op jit(solution)/shard_map/reduce_scatter | solution.py:241
  (436 shorter events, 266.4 us)
Async XLA Ops:
  7.2 61.3 %all-gather.27.cloned.1.call-start = ((), (), s32[]{:S(2)}) async-start(), calls=%async_computation.16 | async-start | bytes 1966080 | tf_op jit(solution)/shard_map/all_gather | solution.py:115
  31.9 85.5 %reduce-scatter.21.cloned.1.call-start = ((), (), s32[]{:S(2)}) async-start(), calls=%async_computation.17 | async-start | bytes 1966080 | tf_op jit(solution)/shard_map/reduce_scatter | solution.py:123
  83.0 73.7 %all-gather.29.cloned.1.call-start = ((), (), s32[]{:S(2)}) async-start(), calls=%async_computation.18 | async-start | bytes 1966080 | tf_op jit(solution)/shard_map/all_gather | solution.py:130
  120.6 76.3 %all-gather.45.cloned.1.call-start = ((), (), s32[]{:S(2)}) async-start(), calls=%async_computation.39 | async-start | bytes 5308416 | tf_op jit(solution)/shard_map/all_gather | solution.py:110
  122.0 116.1 %all-gather.43.cloned.1.call-start = ((), (), s32[]{:S(2)}) async-start(), calls=%async_computation.38 | async-start | bytes 5308416 | tf_op jit(solution)/shard_map/all_gather | solution.py:109
  124.6 162.8 %reduce-scatter.23.cloned.1.call-start = ((), (), s32[]{:S(2)}) async-start(), calls=%async_computation.19 | async-start | bytes 1966080 | tf_op jit(solution)/shard_map/reduce_scatter | solution.py:140
  133.4 115.5 %copy-start.72 = (pred[1024]{0:T(1024)(128)(4,1)}, pred[1024]{0:T(1024)(128)(4,1)S(1)}, u32[]{:S(2)}) copy-start(pred[1024]{0:T(1024)(128)(4,1)S(1)} %broadcast_compare_fusion) | copy-start | bytes 3076
  165.7 72.5 %copy-start.5 = (bf16[4,256,768]{1,2,0:T(8,128)(2,1)}, bf16[4,256,768]{1,2,0:T(8,128)(2,1)S(1)}, u32[]{:S(2)}) copy-start(bf16[4,256,768]{1,2,0:T(8,128)(2,1)S(1)} %copy.93) | copy-start | bytes 4718596
  252.0 74.0 %all-gather.31.cloned.1.call-start = ((), (), s32[]{:S(2)}) async-start(), calls=%async_computation.20 | async-start | bytes 1966080 | tf_op jit(solution)/shard_map/all_gather | solution.py:115
  262.7 42.8 %copy-start.65 = (f32[768]{0:T(1024)}, f32[768]{0:T(1024)S(1)}, u32[]{:S(2)}) copy-start(f32[768]{0:T(1024)S(1)} %convert_element_type.280) | copy-start | bytes 9220
  289.7 85.4 %reduce-scatter.25.cloned.1.call-start = ((), (), s32[]{:S(2)}) async-start(), calls=%async_computation.21 | async-start | bytes 1966080 | tf_op jit(solution)/shard_map/reduce_scatter | solution.py:123
  340.9 74.7 %all-gather.49.cloned.1.call-start = ((), (), s32[]{:S(2)}) async-start(), calls=%async_computation.41 | async-start | bytes 5308416 | tf_op jit(solution)/shard_map/all_gather | solution.py:110
  342.2 111.9 %all-gather.33.cloned.1.call-start = ((), (), s32[]{:S(2)}) async-start(), calls=%async_computation.22 | async-start | bytes 1966080 | tf_op jit(solution)/shard_map/all_gather | solution.py:130
  376.4 47.7 %copy-start.99 = (f32[256]{0:T(256)}, f32[256]{0:T(256)S(1)}, u32[]{:S(2)}) copy-start(f32[256]{0:T(256)S(1)} %multiply_reduce_fusion.8) | copy-start | bytes 3076
  376.4 272.9 %copy-start.75 = (f32[256]{0:T(256)}, f32[256]{0:T(256)S(1)}, u32[]{:S(2)}) copy-start(f32[256]{0:T(256)S(1)} %fusion.171) | copy-start | bytes 3076
  378.3 116.1 %all-gather.47.cloned.1.call-start = ((), (), s32[]{:S(2)}) async-start(), calls=%async_computation.40 | async-start | bytes 5308416 | tf_op jit(solution)/shard_map/all_gather | solution.py:109
  379.0 167.9 %reduce-scatter.27.cloned.1.call-start = ((), (), s32[]{:S(2)}) async-start(), calls=%async_computation.23 | async-start | bytes 1966080 | tf_op jit(solution)/shard_map/reduce_scatter | solution.py:140
  511.4 73.7 %all-gather.35.cloned.1.call-start = ((), (), s32[]{:S(2)}) async-start(), calls=%async_computation.24 | async-start | bytes 1966080 | tf_op jit(solution)/shard_map/all_gather | solution.py:194
  521.8 93.6 %copy-start.86 = (f32[256]{0:T(256)}, f32[256]{0:T(256)S(1)}, u32[]{:S(2)}) copy-start(f32[256]{0:T(256)S(1)} %get-tuple-element.152) | copy-start | bytes 3076
  521.8 127.4 %copy-start.67 = (f32[256,4]{0,1:T(4,128)}, f32[256,4]{0,1:T(4,128)S(1)}, u32[]{:S(2)}) copy-start(f32[256,4]{0,1:T(4,128)S(1)} %get-tuple-element.153) | copy-start | bytes 12292
  548.9 100.4 %reduce-scatter.29.cloned.1.call-start = ((), (), s32[]{:S(2)}) async-start(), calls=%async_computation.25 | async-start | bytes 1966080 | tf_op jit(solution)/shard_map/reduce_scatter | solution.py:208
  614.9 74.7 %all-gather.37.cloned.1.call-start = ((), (), s32[]{:S(2)}) async-start(), calls=%async_computation.26 | async-start | bytes 1966080 | tf_op jit(solution)/shard_map/all_gather | solution.py:217
  653.4 135.4 %reduce-scatter.31.cloned.1.call-start = ((), (), s32[]{:S(2)}) async-start(), calls=%async_computation.27 | async-start | bytes 1966080 | tf_op jit(solution)/shard_map/reduce_scatter | solution.py:229
  705.1 45.3 %copy-start.47 = (bf16[3,64,1024]{2,1,0:T(8,128)(2,1)}, bf16[3,64,1024]{2,1,0:T(8,128)(2,1)S(1)}, u32[]{:S(2)}) copy-start(bf16[3,64,1024]{2,1,0:T(8,128)(2,1)S(1)} %fusion.84) | copy-start | bytes 1179652
  750.4 40.2 %copy-start.98 = (f32[256]{0:T(256)S(1)}, f32[256]{0:T(256)}, u32[]{:S(2)}) copy-start(f32[256]{0:T(256)} %copy-done.97) | copy-start | bytes 3076
  750.4 40.2 %copy-start.22 = (bf16[256,768]{1,0:T(8,128)(2,1)S(1)}, bf16[256,768]{1,0:T(8,128)(2,1)}, u32[]{:S(2)}) copy-start(bf16[256,768]{1,0:T(8,128)(2,1)} %param.12) | copy-start | bytes 1179652
  754.5 77.4 %all-gather.39.cloned.1.call-start = ((), (), s32[]{:S(2)}) async-start(), calls=%async_computation.28 | async-start | bytes 1966080 | tf_op jit(solution)/shard_map/all_gather | solution.py:194
  795.6 100.5 %reduce-scatter.33.cloned.1.call-start = ((), (), s32[]{:S(2)}) async-start(), calls=%async_computation.29 | async-start | bytes 1966080 | tf_op jit(solution)/shard_map/reduce_scatter | solution.py:208
  861.8 74.1 %all-gather.41.cloned.1.call-start = ((), (), s32[]{:S(2)}) async-start(), calls=%async_computation.30 | async-start | bytes 1966080 | tf_op jit(solution)/shard_map/all_gather | solution.py:217
  899.7 161.4 %reduce-scatter.51.cloned.1.call-start = ((), (), s32[]{:S(2)}) async-start(), calls=%async_computation.43 | async-start | bytes 442368
  901.8 160.2 %reduce-scatter.49.cloned.1.call-start = ((), (), s32[]{:S(2)}) async-start(), calls=%async_computation.42 | async-start | bytes 442368
  903.9 158.9 %reduce-scatter.43.cloned.1.call-start = ((), (), s32[]{:S(2)}) async-start(), calls=%async_computation.35 | async-start | bytes 884736 | tf_op jit(solution)/shard_map/reduce_scatter | solution.py:236
  907.1 177.8 %reduce-scatter.41.cloned.1.call-start = ((), (), s32[]{:S(2)}) async-start(), calls=%async_computation.34 | async-start | bytes 884736 | tf_op jit(solution)/shard_map/reduce_scatter | solution.py:236
  938.9 192.3 %reduce-scatter.39.cloned.1.call-start = ((), (), s32[]{:S(2)}) async-start(), calls=%async_computation.33 | async-start | bytes 2654208 | tf_op jit(solution)/shard_map/reduce_scatter | solution.py:235
  943.4 234.5 %reduce-scatter.37.cloned.1.call-start = ((), (), s32[]{:S(2)}) async-start(), calls=%async_computation.32 | async-start | bytes 2654208 | tf_op jit(solution)/shard_map/reduce_scatter | solution.py:235
  1001.3 214.2 %reduce-scatter.35.cloned.1.call-start = ((), (), s32[]{:S(2)}) async-start(), calls=%async_computation.31 | async-start | bytes 1966080 | tf_op jit(solution)/shard_map/reduce_scatter | solution.py:229
  1005.6 452.8 %all-reduce.16.cloned.1.call-start = ((), (), s32[]{:S(2)}) async-start(), calls=%async_computation.44 | async-start | bytes 37748736
  1043.4 495.5 %reduce-scatter.47.cloned.1.call-start = ((), (), s32[]{:S(2)}) async-start(), calls=%async_computation.37 | async-start | bytes 10616832 | tf_op jit(solution)/shard_map/reduce_scatter | solution.py:241
  1051.9 567.4 %reduce-scatter.45.cloned.1.call-start = ((), (), s32[]{:S(2)}) async-start(), calls=%async_computation.36 | async-start | bytes 10616832 | tf_op jit(solution)/shard_map/reduce_scatter | solution.py:241
  1060.3 155.2 %copy-start.62 = (f32[768]{0:T(1024)S(1)}, f32[768]{0:T(1024)}, u32[]{:S(2)}) copy-start(f32[768]{0:T(1024)} %copy-done.61) | copy-start | bytes 9220
  1060.3 155.2 %copy-start.85 = (f32[256]{0:T(256)S(1)}, f32[256]{0:T(256)}, u32[]{:S(2)}) copy-start(f32[256]{0:T(256)} %copy-done.84) | copy-start | bytes 3076
  1060.3 156.5 %copy-start.79 = (f32[768]{0:T(1024)S(1)}, f32[768]{0:T(1024)}, u32[]{:S(2)}) copy-start(f32[768]{0:T(1024)} %get-tuple-element.126) | copy-start | bytes 9220
  1060.3 156.5 %copy-start.80 = (f32[768]{0:T(1024)S(1)}, f32[768]{0:T(1024)}, u32[]{:S(2)}) copy-start(f32[768]{0:T(1024)} %get-tuple-element.130) | copy-start | bytes 9220
  1060.3 156.5 %copy-start.107 = (f32[768]{0:T(1024)S(1)}, f32[768]{0:T(1024)}, u32[]{:S(2)}) copy-start(f32[768]{0:T(1024)} %get-tuple-element.128) | copy-start | bytes 9220
  1060.3 193.2 %copy-start.94 = (f32[256]{0:T(256)S(1)}, f32[256]{0:T(256)}, u32[]{:S(2)}) copy-start(f32[256]{0:T(256)} %copy-done.93) | copy-start | bytes 3076
  1060.3 193.2 %copy-start.89 = (f32[256]{0:T(256)S(1)}, f32[256]{0:T(256)}, u32[]{:S(2)}) copy-start(f32[256]{0:T(256)} %copy-done.87) | copy-start | bytes 3076
  1060.3 193.2 %copy-start.102 = (f32[256]{0:T(256)S(1)}, f32[256]{0:T(256)}, u32[]{:S(2)}) copy-start(f32[256]{0:T(256)} %copy-done.101) | copy-start | bytes 3076
  1060.3 193.2 %copy-start.24 = (f32[256,768]{1,0:T(8,128)S(1)}, f32[256,768]{1,0:T(8,128)}, u32[]{:S(2)}) copy-start(f32[256,768]{1,0:T(8,128)} %copy-done.23) | copy-start | bytes 2359300
  (96 other events, 1496.7 us)
Sparse Core Ops, SparseCore 0:
  32.0 36.4 all-gather.26
  83.2 34.1 reduce-scatter.20
  120.7 36.0 all-gather.28
  159.1 37.7 all-gather.44
  199.2 38.9 all-gather.42
  252.1 35.2 reduce-scatter.22
  289.9 36.0 all-gather.30
  341.0 34.1 reduce-scatter.24
  377.6 37.8 all-gather.48
  417.0 37.0 all-gather.32
  456.6 37.7 all-gather.46
  511.6 35.2 reduce-scatter.26
  549.0 36.0 all-gather.34
  615.0 34.1 reduce-scatter.28
  653.5 36.0 all-gather.36
  754.6 34.1 reduce-scatter.30
  795.7 36.0 all-gather.38
  862.0 34.1 reduce-scatter.32
  899.8 36.0 all-gather.40
  938.8 32.7 reduce-scatter.50
  974.6 33.8 reduce-scatter.48
  1011.7 34.9 reduce-scatter.42
  1049.8 34.9 reduce-scatter.40
  1088.7 42.4 reduce-scatter.38
  1135.5 42.4 reduce-scatter.36
  1180.1 35.2 reduce-scatter.34
  1219.2 239.0 all-reduce.15
  1462.3 76.5 reduce-scatter.46
  1542.8 76.4 reduce-scatter.44
where the time goes:
time: 1640 us; the launch traced here: 1630 us
  waiting for transfers between devices  1070 us (65%)
  matrix products  228 us (14%)
  local copies, waits for them, and re-layouts  144 us (9%)
  blocking collectives  114 us (7%)
  other arithmetic  52.7 us (3%)
  between operations  17.6 us (1%)
    unnamed x32, waiting for transfers between devices  204 us
    reduce_scatter x2, waiting for transfers between devices, local(): lax.psum_scatter(grad_down, 'fsdp', scatter_dimension=0, tiled=True)  157 us
    reduce_scatter x2, waiting for transfers between devices, local(): lax.psum_scatter(grad_qkv, 'fsdp', scatter_dimension=0, tiled=True)  91.3 us
    all_gather x2, waiting for transfers between devices, local(): d_comb_rows = lax.all_gather(d_combined, 'tp', axis=0, tiled=True)  72.4 us
    reduce_scatter x2, waiting for transfers between devices, local(): lax.psum_scatter(d_a_rows.astype(jnp.bfloat16), 'tp', scatter_dimension=0...  69.8 us
    reduce_scatter x2, waiting for transfers between devices, local(): lax.psum_scatter(d_tokens.astype(jnp.bfloat16), 'tp', scatter_dimension=0...  68 us
    all_gather x2, waiting for transfers between devices, local(): lax.all_gather(down_weight[layer_index], 'fsdp', axis=2, tiled=True)  67.5 us
    reduce_scatter x2, waiting for transfers between devices, local(): lax.psum_scatter(partial_attn.astype(jnp.bfloat16), 'tp', scatter_dimensi...  67.1 us
  transfers between devices with their start and end apart: 29, of which 26 were waited for; matrix products, arithmetic and copies ran while one was open for 12% of the time, Pallas kernels for 0%

commit v1 on v0

v1 whole, which is shorter than its diff:
```python
import jax
import jax.numpy as jnp
from jax import lax
from jax.experimental import pallas as pl
from jax.experimental.pallas import tpu as pltpu
from jax.sharding import PartitionSpec as P

DH = 64
LAYERS = 2
BLOCK = 256

EPSILON = 1e-06
HIGH = lax.Precision.HIGHEST
BF = jnp.bfloat16
F32 = jnp.float32
GELU_C = 0.7978845608028654
GELU_A = 0.044715
VMEM_BYTES = 48 * 1024 * 1024


def dot(left, right, left_dim, right_dim):
    return lax.dot_general(
        left, right, (((left_dim,), (right_dim,)), ((), ())), preferred_element_type=F32
    )


def normed(hidden, gain_row):
    scale_inv = lax.rsqrt(jnp.mean(hidden * hidden, -1, keepdims=True) + EPSILON)
    return hidden * scale_inv * gain_row


def normed_back(hidden, gain_row, upstream):
    _, pull_back = jax.vjp(normed, hidden, gain_row)
    return pull_back(upstream)


def params():
    return pltpu.CompilerParams(
        dimension_semantics=("arbitrary",), vmem_limit_bytes=VMEM_BYTES
    )


def whole_spec(array):
    rank = len(array.shape)
    return pl.BlockSpec(array.shape, lambda i: (0,) * rank)


def attend_ahead_body(a_ref, w_ref, part_ref, qkv_ref, mixed_ref):
    step = pl.program_id(0)
    heads_dim = mixed_ref.shape[1]
    heads = heads_dim // DH

    @pl.when(step == 0)
    def _():
        qkv_ref[...] = dot(a_ref[...], w_ref[:, : 3 * heads_dim], 1, 0).astype(BF)

    rows = pl.ds(pl.multiple_of(step * BLOCK, BLOCK), BLOCK)
    parts = []
    for head in range(heads):
        low = head * DH
        query = qkv_ref[rows, low : low + DH] * BF(DH**-0.5)
        key_rows = qkv_ref[:, heads_dim + low : heads_dim + low + DH]
        value_rows = qkv_ref[:, 2 * heads_dim + low : 2 * heads_dim + low + DH]
        scores = dot(query, key_rows, 1, 1)
        expon = jnp.exp(scores - jnp.max(scores, -1, keepdims=True))
        total = jnp.sum(expon, -1, keepdims=True)
        probs = (expon * (1.0 / total)).astype(BF)
        parts.append(dot(probs, value_rows, 1, 0))
    mixed = jnp.concatenate(parts, -1).astype(BF)
    mixed_ref[...] = mixed
    part_ref[...] = dot(mixed, w_ref[:, 3 * heads_dim : 4 * heads_dim], 1, 1).astype(BF)


def attend_ahead(a_rows, w_pack, heads_dim):
    tokens, width = a_rows.shape
    return pl.pallas_call(
        attend_ahead_body,
        grid=(tokens // BLOCK,),
        in_specs=[whole_spec(a_rows), whole_spec(w_pack)],
        out_specs=[
            pl.BlockSpec((BLOCK, width), lambda i: (i, 0)),
            pl.BlockSpec((tokens, 3 * heads_dim), lambda i: (0, 0)),
            pl.BlockSpec((BLOCK, heads_dim), lambda i: (i, 0)),
        ],
        out_shape=[
            jax.ShapeDtypeStruct((tokens, width), BF),
            jax.ShapeDtypeStruct((tokens, 3 * heads_dim), BF),
            jax.ShapeDtypeStruct((tokens, heads_dim), BF),
        ],
        compiler_params=params(),
        cost_estimate=pl.CostEstimate(
            flops=2 * tokens * heads_dim * (4 * width + 4 * 2 * tokens),
            bytes_accessed=8 * 1024 * 1024,
            transcendentals=tokens * tokens * heads_dim // DH,
        ),
    )(a_rows, w_pack)


def attend_behind_body(
    da_ref, a_ref, qkv_ref, mixed_ref, w_ref, back_ref, grad_ref, dqkv_ref, acc_ref
):
    step = pl.program_id(0)
    heads_dim = mixed_ref.shape[1]
    heads = heads_dim // DH

    @pl.when(step == 0)
    def _():
        acc_ref[...] = jnp.zeros_like(acc_ref)

    rows = pl.ds(pl.multiple_of(step * BLOCK, BLOCK), BLOCK)
    d_mixed = dot(da_ref[rows, :], w_ref[:, 3 * heads_dim : 4 * heads_dim], 1, 0).astype(BF)
    query_parts = []
    key_parts = []
    value_parts = []
    for head in range(heads):
        low = head * DH
        query = qkv_ref[rows, low : low + DH]
        key_rows = qkv_ref[:, heads_dim + low : heads_dim + low + DH]
        value_rows = qkv_ref[:, 2 * heads_dim + low : 2 * heads_dim + low + DH]
        d_mixed_one = d_mixed[:, low : low + DH]
        scores = dot(key_rows, query * BF(DH**-0.5), 1, 1)
        expon = jnp.exp(scores - jnp.max(scores, 0, keepdims=True))
        probs = expon * (1.0 / jnp.sum(expon, 0, keepdims=True))
        d_probs = dot(value_rows, d_mixed_one, 1, 1)
        weighted = probs * d_probs
        d_scores = weighted - probs * jnp.sum(weighted, 0, keepdims=True)
        d_scaled = (d_scores * (DH**-0.5)).astype(BF)
        query_parts.append(dot(d_scaled, key_rows, 0, 0))
        key_parts.append(dot(d_scaled, query, 1, 0))
        value_parts.append(dot(probs.astype(BF), d_mixed_one, 1, 0))
    dqkv_ref[rows, :heads_dim] = jnp.concatenate(query_parts, -1).astype(BF)
    acc_ref[...] += jnp.concatenate(key_parts + value_parts, -1)

    @pl.when(step == pl.num_programs(0) - 1)
    def _():
        dqkv_ref[:, heads_dim:] = acc_ref[...].astype(BF)
        back_ref[...] = dot(dqkv_ref[...], w_ref[:, : 3 * heads_dim], 1, 1).astype(BF)
        grad_ref[:, : 3 * heads_dim] = dot(a_ref[...], dqkv_ref[...], 0, 0).astype(BF)
        grad_ref[:, 3 * heads_dim :] = dot(da_ref[...], mixed_ref[...], 0, 0).astype(BF)


def attend_behind(da_rows, a_rows, qkv, mixed, w_pack):
    tokens, width = a_rows.shape
    heads_dim = mixed.shape[1]
    operands = (da_rows, a_rows, qkv, mixed, w_pack)
    return pl.pallas_call(
        attend_behind_body,
        grid=(tokens // BLOCK,),
        in_specs=[whole_spec(operand) for operand in operands],
        out_specs=[
            pl.BlockSpec((tokens, width), lambda i: (0, 0)),
            pl.BlockSpec((width, 4 * heads_dim), lambda i: (0, 0)),
        ],
        out_shape=[
            jax.ShapeDtypeStruct((tokens, width), BF),
            jax.ShapeDtypeStruct((width, 4 * heads_dim), BF),
        ],
        scratch_shapes=[
            pltpu.VMEM((tokens, 3 * heads_dim), BF),
            pltpu.VMEM((tokens, 2 * heads_dim), F32),
        ],
        compiler_params=params(),
        cost_estimate=pl.CostEstimate(
            flops=2 * tokens * heads_dim * (8 * width + 4 * 5 * tokens),
            bytes_accessed=10 * 1024 * 1024,
            transcendentals=tokens * tokens * heads_dim // DH,
        ),
    )(*operands)


def pick_rows(position_ref, step, capacity):
    tokens = position_ref.shape[1]
    slot = lax.broadcasted_iota(jnp.int32, (capacity, tokens), 0) + step * capacity
    return jnp.where(slot == position_ref[...], 1.0, 0.0).astype(BF)


def place_rows(position_ref, slots_total):
    tokens = position_ref.shape[0]
    slot = lax.broadcasted_iota(jnp.int32, (tokens, slots_total), 1)
    return jnp.where(slot == position_ref[...], 1.0, 0.0).astype(BF)


def experts_ahead_body(b_ref, row_ref, col_ref, w_ref, out_ref, buffer_ref, pre_ref, eo_ref):
    step = pl.program_id(0)
    capacity, hidden = pre_ref.shape
    buffer = dot(pick_rows(row_ref, step, capacity), b_ref[...], 1, 0).astype(BF)
    buffer_ref[...] = buffer
    pre = dot(buffer, w_ref[:, :hidden], 1, 0)
    pre_ref[...] = pre
    act = (0.5 * pre * (1.0 + jnp.tanh(GELU_C * (pre + GELU_A * pre * pre * pre)))).astype(BF)
    rows = pl.ds(pl.multiple_of(step * capacity, capacity), capacity)
    eo_ref[rows, :] = dot(act, w_ref[:, hidden:], 1, 1).astype(BF)

    @pl.when(step == pl.num_programs(0) - 1)
    def _():
        place = place_rows(col_ref, eo_ref.shape[0])
        out_ref[...] = dot(place, eo_ref[...], 1, 0).astype(BF)


def experts_ahead(b_rows, pos_row, pos_col, w_pack, experts, capacity):
    tokens, width = b_rows.shape
    both = w_pack.shape[1] // experts
    hidden = both // 2
    slots_total = experts * capacity
    return pl.pallas_call(
        experts_ahead_body,
        grid=(experts,),
        in_specs=[
            whole_spec(b_rows),
            whole_spec(pos_row),
            whole_spec(pos_col),
            pl.BlockSpec((width, both), lambda i: (0, i)),
        ],
        out_specs=[
            pl.BlockSpec((tokens, width), lambda i: (0, 0)),
            pl.BlockSpec((capacity, width), lambda i: (i, 0)),
            pl.BlockSpec((capacity, hidden), lambda i: (i, 0)),
        ],
        out_shape=[
            jax.ShapeDtypeStruct((tokens, width), BF),
            jax.ShapeDtypeStruct((slots_total, width), BF),
            jax.ShapeDtypeStruct((slots_total, hidden), F32),
        ],
        scratch_shapes=[pltpu.VMEM((slots_total, width), BF)],
        compiler_params=params(),
        cost_estimate=pl.CostEstimate(
            flops=2 * slots_total * width * (2 * hidden + 2 * tokens),
            bytes_accessed=20 * 1024 * 1024,
            transcendentals=slots_total * hidden,
        ),
    )(b_rows, pos_row, pos_col, w_pack)


def experts_behind_body(
    dc_ref, row_ref, col_ref, buffer_ref, pre_ref, w_ref, back_ref, grad_ref, db_ref
):
    step = pl.program_id(0)
    capacity, hidden = pre_ref.shape
    d_out = dot(pick_rows(row_ref, step, capacity), dc_ref[...], 1, 0).astype(BF)
    pre = pre_ref[...]
    squared = pre * pre
    bent = jnp.tanh(GELU_C * (pre + GELU_A * squared * pre))
    half = 0.5 * (1.0 + bent)
    act = (pre * half).astype(BF)
    grad_ref[:, hidden:] = dot(d_out, act, 0, 0).astype(BF)
    slope = half + 0.5 * pre * (1.0 - bent * bent) * (GELU_C * (1.0 + 3.0 * GELU_A * squared))
    d_pre = (dot(d_out, w_ref[:, hidden:], 1, 0) * slope).astype(BF)
    grad_ref[:, :hidden] = dot(buffer_ref[...], d_pre, 0, 0).astype(BF)
    rows = pl.ds(pl.multiple_of(step * capacity, capacity), capacity)
    db_ref[rows, :] = dot(d_pre, w_ref[:, :hidden], 1, 1).astype(BF)

    @pl.when(step == pl.num_programs(0) - 1)
    def _():
        place = place_rows(col_ref, db_ref.shape[0])
        back_ref[...] = dot(place, db_ref[...], 1, 0).astype(BF)


def experts_behind(dc_rows, pos_row, pos_col, buffer, pre, w_pack, experts, capacity):
    tokens, width = dc_rows.shape
    both = w_pack.shape[1] // experts
    hidden = both // 2
    slots_total = experts * capacity
    return pl.pallas_call(
        experts_behind_body,
        grid=(experts,),
        in_specs=[
            whole_spec(dc_rows),
            whole_spec(pos_row),
            whole_spec(pos_col),
            pl.BlockSpec((capacity, width), lambda i: (i, 0)),
            pl.BlockSpec((capacity, hidden), lambda i: (i, 0)),
            pl.BlockSpec((width, both), lambda i: (0, i)),
        ],
        out_specs=[
            pl.BlockSpec((tokens, width), lambda i: (0, 0)),
            pl.BlockSpec((width, both), lambda i: (0, i)),
        ],
        out_shape=[
            jax.ShapeDtypeStruct((tokens, width), BF),
            jax.ShapeDtypeStruct((width, experts * both), BF),
        ],
        scratch_shapes=[pltpu.VMEM((slots_total, width), BF)],
        compiler_params=params(),
        cost_estimate=pl.CostEstimate(
            flops=2 * slots_total * width * (4 * hidden + 2 * tokens),
            bytes_accessed=30 * 1024 * 1024,
            transcendentals=slots_total * hidden,
        ),
    )(dc_rows, pos_row, pos_col, buffer, pre, w_pack)


def gather_tokens(part):
    return lax.all_gather(part, "tp", axis=0, tiled=True)


def scatter_tokens(whole):
    return lax.psum_scatter(whole, "tp", scatter_dimension=0, tiled=True).astype(F32)


def local(
    inputs,
    cotangent,
    qkv_weight,
    out_weight,
    attn_gain,
    ffn_gain,
    router_weight,
    in_weight,
    down_weight,
    routes,
    slots,
):
    tp_index = lax.axis_index("tp")
    fsdp_index = lax.axis_index("fsdp")
    tok_here, width = inputs.shape
    shard = in_weight.shape[2]
    experts = in_weight.shape[1]
    hidden_units = in_weight.shape[3]
    heads_dim = qkv_weight.shape[3]
    group_tok = routes.shape[0]
    capacity = group_tok // experts

    packs = []
    for layer_index in range(LAYERS):
        small = [
            jnp.transpose(qkv_weight[layer_index], (1, 0, 2)).reshape(shard, 3 * heads_dim),
            out_weight[layer_index].T,
            attn_gain[layer_index][:, None],
            ffn_gain[layer_index][:, None],
            router_weight[layer_index],
        ]
        columns = 4 * heads_dim + 2 + experts
        small.append(jnp.zeros((shard, -columns % 128), BF))
        large = jnp.stack(
            [in_weight[layer_index], jnp.transpose(down_weight[layer_index], (0, 2, 1))], 1
        )
        large = jnp.transpose(large, (2, 0, 1, 3)).reshape(shard, experts * 2 * hidden_units)
        packs.append(
            (
                lax.all_gather(jnp.concatenate(small, 1), "fsdp", axis=0, tiled=True),
                lax.all_gather(large, "fsdp", axis=0, tiled=True),
            )
        )

    position = jnp.where(slots < capacity, routes * capacity + slots, -1)
    pos_row, pos_col = position[None, :], position[:, None]
    route_here = lax.dynamic_slice_in_dim(routes, tp_index * tok_here, tok_here)
    pick = (route_here[:, None] == jnp.arange(experts, dtype=jnp.int32)[None, :]).astype(F32)
    hidden = inputs.astype(F32)
    saved = []
    for layer_index in range(LAYERS):
        w_attn, w_experts = packs[layer_index]
        rest = w_attn[:, 4 * heads_dim : 4 * heads_dim + 2 + experts]
        rest_rows = rest.astype(F32).T
        gain_one, gain_two, router_rows = rest_rows[0], rest_rows[1], rest_rows[2:]
        a_here = normed(hidden, gain_one).astype(BF)
        a_rows = gather_tokens(a_here)
        partial_attn, qkv, mixed = attend_ahead(a_rows, w_attn, heads_dim)
        middle = hidden + scatter_tokens(partial_attn)
        b_here = normed(middle, gain_two).astype(BF)
        b_rows = gather_tokens(b_here)
        logits = jnp.dot(b_here, rest[:, 2:], preferred_element_type=F32)
        probs = jax.nn.softmax(logits, -1)
        gate = jnp.sum(probs * pick, -1)
        token_out, buffer, pre = experts_ahead(
            b_rows, pos_row, pos_col, w_experts, experts, capacity
        )
        combined = scatter_tokens(token_out)
        saved.append(
            (gain_one, gain_two, router_rows, hidden, a_rows, qkv, mixed, middle)
            + (b_here, probs, gate, combined, buffer, pre)
        )
        hidden = middle + gate[:, None] * combined
    upstream = cotangent.astype(F32)
    layer_grads = [None] * LAYERS
    small_sums = [None] * LAYERS
    for layer_index in reversed(range(LAYERS)):
        w_attn, w_experts = packs[layer_index]
        (gain_one, gain_two, router_rows, before, a_rows, qkv, mixed, middle) = saved[layer_index][:8]
        (b_here, probs, gate, combined, buffer, pre) = saved[layer_index][8:]
        dc_rows = gather_tokens((gate[:, None] * upstream).astype(BF))
        d_gate = jnp.sum(upstream * combined, -1)
        d_tokens, grad_experts = experts_behind(
            dc_rows, pos_row, pos_col, buffer, pre, w_experts, experts, capacity
        )
        d_logits = d_gate[:, None] * gate[:, None] * (pick - probs)
        d_b_here = scatter_tokens(d_tokens)
        for expert in range(experts):
            d_b_here = d_b_here + d_logits[:, expert : expert + 1] * router_rows[expert][None, :]
        grad_router = lax.dot_general(
            d_logits, b_here.astype(F32), (((0,), (0,)), ((), ())), precision=HIGH
        )
        d_middle, grad_gain_two = normed_back(middle, gain_two, d_b_here)
        d_middle = d_middle + upstream
        da_rows = gather_tokens(d_middle.astype(BF))
        d_a_rows, grad_attn = attend_behind(da_rows, a_rows, qkv, mixed, w_attn)
        d_before, grad_gain_one = normed_back(before, gain_one, scatter_tokens(d_a_rows))
        upstream = d_before + d_middle
        layer_grads[layer_index] = (
            lax.psum_scatter(grad_attn, "fsdp", scatter_dimension=0, tiled=True),
            lax.psum_scatter(grad_experts, "fsdp", scatter_dimension=0, tiled=True),
        )
        small_sums[layer_index] = jnp.concatenate(
            [grad_gain_one[None], grad_gain_two[None], grad_router], 0
        )
    sums = lax.psum(jnp.concatenate(small_sums, 0), ("fsdp", "tp"))
    sums = lax.dynamic_slice_in_dim(sums, fsdp_index * shard, shard, 1)
    sums = sums.reshape(LAYERS, 2 + experts, shard)
    attn_grads = jnp.stack([grads[0] for grads in layer_grads]).astype(F32)
    expert_grads = jnp.stack([grads[1] for grads in layer_grads]).astype(F32)
    expert_grads = expert_grads.reshape(LAYERS, shard, experts, 2, hidden_units)
    qkv_grads = attn_grads[:, :, : 3 * heads_dim].reshape(LAYERS, shard, 3, heads_dim)
    return (
        hidden,
        upstream,
        jnp.transpose(qkv_grads, (0, 2, 1, 3)),
        jnp.transpose(attn_grads[:, :, 3 * heads_dim :], (0, 2, 1)),
        sums[:, 0],
        sums[:, 1],
        jnp.transpose(sums[:, 2:], (0, 2, 1)),
        jnp.transpose(expert_grads[:, :, :, 0], (0, 2, 1, 3)),
        jnp.transpose(expert_grads[:, :, :, 1], (0, 2, 3, 1)),
    )


def solution(mesh):
    return jax.shard_map(
        local,
        mesh=mesh,
        in_specs=(
            P(("fsdp", "tp"), None),
            P(("fsdp", "tp"), None),
            P(None, None, "fsdp", "tp"),
            P(None, "tp", "fsdp"),
            P(None, "fsdp"),
            P(None, "fsdp"),
            P(None, "fsdp", None),
            P(None, None, "fsdp", "tp"),
            P(None, None, "tp", "fsdp"),
            P("fsdp"),
            P("fsdp"),
        ),
        out_specs=(
            P(("fsdp", "tp"), None),
            P(("fsdp", "tp"), None),
            P(None, None, "fsdp", "tp"),
            P(None, "tp", "fsdp"),
            P(None, "fsdp"),
            P(None, "fsdp"),
            P(None, "fsdp", None),
            P(None, None, "fsdp", "tp"),
            P(None, None, "tp", "fsdp"),
        ),
        check_vma=False,
    )
```

time: 1640 us -> 1160 us (0.71)
  matrix products: 228 us -> 2.29 us
  waiting for transfers between devices: 1070 us -> 877 us
  Pallas kernels: 0 us -> 127 us
  local copies, waits for them, and re-layouts: 144 us -> 52.1 us
  blocking collectives: 114 us -> 39.8 us
  other arithmetic: 52.7 us -> 32.2 us
    dot_general x38 -> x4, matrix products: 219 us -> 2.29 us  [the longest x2 1.74 us: local(): logits = jnp.dot(b_here, rest[:, 2:], preferred_element_type=F32)]
    unnamed x32 -> x24, waiting for transfers between devices: 204 us -> 2.7 us
    pallas_call x0 -> x8, Pallas kernels: none -> 127 us  [the longest x2 47.1 us: attend_behind(): pl.pallas_call(attend_behind_body, grid=(tokens // BLOCK,), in_specs=[who...]
    all_gather x12, waiting for transfers between devices: 344 us -> 441 us  [the longest x8 284 us: gather_tokens(): return lax.all_gather(part, 'tp', axis=0, tiled=True)]
    reduce_scatter x14 -> x12, waiting for transfers between devices: 524 us -> 434 us  [the longest x8 267 us: scatter_tokens(): lax.psum_scatter(whole, 'tp', scatter_dimension=0, tiled=True).astype(F32)]
    all_gather x6 -> x0, blocking collectives: 63.4 us -> none  [the longest x2 25.8 us: local(): lax.all_gather(qkv_weight[layer_index], 'fsdp', axis=1, tiled=True)]
    gather x12 -> x0, local copies, waits for them, and re-layouts: 56.7 us -> none  [the longest x4 17.9 us: local(): d_comb_rows[token_of]]
    unnamed x2 -> x0, blocking collectives: 40.9 us -> none
  transfers between devices with their start and end apart: 29 -> 24, of which waited for: 26 -> 24; matrix products, arithmetic and copies ran while one was open for 12% -> 3% of each run, Pallas kernels for 0% -> 3%
where the time goes in v1:
time: 1160 us; the launch traced here: 1150 us
  waiting for transfers between devices  877 us (76%)
  Pallas kernels  127 us (11%)
  local copies, waits for them, and re-layouts  52.1 us (4%)
  blocking collectives  39.8 us (3%)
  other arithmetic  32.2 us (3%)
  between operations  15.1 us (1%)
    all_gather x8, waiting for transfers between devices, gather_tokens(): return lax.all_gather(part, 'tp', axis=0, tiled=True)  284 us
    reduce_scatter x8, waiting for transfers between devices, scatter_tokens(): lax.psum_scatter(whole, 'tp', scatter_dimension=0, tiled=True).astype(F32)  267 us
    all_gather x2, waiting for transfers between devices, local(): lax.all_gather(large, 'fsdp', axis=0, tiled=True)  117 us
    reduce_scatter x2, waiting for transfers between devices, local(): lax.psum_scatter(grad_experts, 'fsdp', scatter_dimension=0, tiled=True)  87.6 us
    reduce_scatter x2, waiting for transfers between devices, local(): lax.psum_scatter(grad_attn, 'fsdp', scatter_dimension=0, tiled=True)  78.8 us
    pallas_call x2, Pallas kernels, attend_behind(): pl.pallas_call(attend_behind_body, grid=(tokens // BLOCK,), in_specs=[who...  47.1 us
    all_gather x2, waiting for transfers between devices, local(): lax.all_gather(jnp.concatenate(small, 1), 'fsdp', axis=0, tiled=True)  40.3 us
    psum x1, blocking collectives, local(): sums = lax.psum(jnp.concatenate(small_sums, 0), ('fsdp', 'tp'))  39.8 us
  transfers between devices with their start and end apart: 24, of which 24 were waited for; matrix products, arithmetic and copies ran while one was open for 3% of the time, Pallas kernels for 3%

profile of v1, /device:TPU:0, one launch (start us, length us, event | category | flops | bytes accessed | tf_op | source)
XLA Modules:
  0.0 1147.7 jit_solution(2285065890921896383)
XLA Ops:
  13.1 27.5 %all-gather.13.cloned.1.call-done.w_ref = bf16[768,896]{1,0:T(8,128)(2,1)} async-done(((bf16[96,896]{1,0:T(8,128)(2,1)}), bf16[768,896]{1,0:T(8,128)(2,1)}) %all-gather.13.cloned.1.call-update) | async-done | bytes 1376272 | tf_op jit(solution)/shard_map/all_gather | solution.py:340
  43.8 37.2 %all-gather.15.cloned.1.call-done.a_ref = bf16[1024,768]{1,0:T(8,128)(2,1)} async-done(((bf16[256,768]{1,0:T(8,128)(2,1)}), bf16[1024,768]{1,0:T(8,128)(2,1)}) %all-gather.15.cloned.1.call-update) | async-done | bytes 1572880 | tf_op jit(solution)/shard_map/all_gather | solution.py:293
  81.0 12.9 %shard_map.178 = (bf16[1024,768]{1,0:T(8,128)(2,1)}, bf16[1024,576]{1,0:T(8,128)(2,1)S(1)}, bf16[1024,192]{1,0:T(8,128)(2,1)S(1)}) custom-call(bf16[1024,768]{1,0:T(8,128)(2,1)} %all-gather.15.cloned.1.call-done.a_ref, bf16[768,896]{1,0:T(8,128)(2,1)S(1)} %copy-done), custom_call_target="tpu_custom_call" | custom-call | flops 4429185024 | bytes 8388608 | tf_op jit(solution)/shard_map/pallas_call | solution.py:76
  95.8 34.3 %reduce-scatter.13.cloned.1.call-done = bf16[256,768]{1,0:T(8,128)(2,1)} async-done(((bf16[1024,768]{1,0:T(8,128)(2,1)}), bf16[256,768]{1,0:T(8,128)(2,1)}) %reduce-scatter.13.cloned.1.call-update) | async-done | bytes 393232 | tf_op jit(solution)/shard_map/reduce_scatter | solution.py:297
  131.3 1.9 multiply_convert_fusion.3
  137.1 1.7 reshape.145
  140.8 28.6 %all-gather.17.cloned.1.call-done.b_ref = bf16[1024,768]{1,0:T(8,128)(2,1)} async-done(((bf16[256,768]{1,0:T(8,128)(2,1)}), bf16[1024,768]{1,0:T(8,128)(2,1)}) %all-gather.17.cloned.1.call-update) | async-done | bytes 1572880 | tf_op jit(solution)/shard_map/all_gather | solution.py:293
  169.4 60.0 %all-gather.19.cloned.1.call-done.w_ref = bf16[768,6144]{1,0:T(8,128)(2,1)} async-done(((bf16[96,6144]{1,0:T(8,128)(2,1)}), bf16[768,6144]{1,0:T(8,128)(2,1)}) %all-gather.19.cloned.1.call-update) | async-done | bytes 9437200 | tf_op jit(solution)/shard_map/all_gather | solution.py:341
  230.9 11.6 %shard_map.179 = (bf16[1024,768]{1,0:T(8,128)(2,1)}, bf16[1024,768]{1,0:T(8,128)(2,1)S(1)}, f32[1024,768]{1,0:T(8,128)}) custom-call(bf16[1024,768]{1,0:T(8,128)(2,1)S(1)} %copy-done.2, s32[1,1024]{1,0:T(1,128)S(1)} %bitcast.86, s32[1024,1]{1,0:T(8,128)S(1)} %copy.43.col_ref, bf16[768,6144]{1,0:T(8,128)(2,1)} %all-gather.19.cloned.1.call-done.w_ref), custom_call_target="tpu_custom_call" | custom-call | flops 5637144576 | bytes 20971520 | tf_op jit(solution)/shard_map/pallas_call | solution.py:205
  243.9 12.8 %all-gather.21.cloned.1.call-done.w_ref = bf16[768,896]{1,0:T(8,128)(2,1)} async-done(((bf16[96,896]{1,0:T(8,128)(2,1)}), bf16[768,896]{1,0:T(8,128)(2,1)}) %all-gather.21.cloned.1.call-update) | async-done | bytes 1376272 | tf_op jit(solution)/shard_map/all_gather | solution.py:340
  259.3 35.6 %reduce-scatter.15.cloned.1.call-done = bf16[256,768]{1,0:T(8,128)(2,1)} async-done(((bf16[1024,768]{1,0:T(8,128)(2,1)}), bf16[256,768]{1,0:T(8,128)(2,1)}) %reduce-scatter.15.cloned.1.call-update) | async-done | bytes 393232 | tf_op jit(solution)/shard_map/reduce_scatter | solution.py:297
  294.9 1.7 multiply_reduce_fusion.5
  298.4 36.2 %all-gather.23.cloned.1.call-done.a_ref = bf16[1024,768]{1,0:T(8,128)(2,1)} async-done(((bf16[256,768]{1,0:T(8,128)(2,1)}), bf16[1024,768]{1,0:T(8,128)(2,1)}) %all-gather.23.cloned.1.call-update) | async-done | bytes 1572880 | tf_op jit(solution)/shard_map/all_gather | solution.py:293
  334.6 12.9 %shard_map.180 = (bf16[1024,768]{1,0:T(8,128)(2,1)}, bf16[1024,576]{1,0:T(8,128)(2,1)S(1)}, bf16[1024,192]{1,0:T(8,128)(2,1)S(1)}) custom-call(bf16[1024,768]{1,0:T(8,128)(2,1)} %all-gather.23.cloned.1.call-done.a_ref, bf16[768,896]{1,0:T(8,128)(2,1)S(1)} %copy-done.1), custom_call_target="tpu_custom_call" | custom-call | flops 4429185024 | bytes 8388608 | tf_op jit(solution)/shard_map/pallas_call | solution.py:76
  349.5 3.5 copy.50
  353.0 2.8 reshape.147
  355.8 27.9 %reduce-scatter.17.cloned.1.call-done = bf16[256,768]{1,0:T(8,128)(2,1)} async-done(((bf16[1024,768]{1,0:T(8,128)(2,1)}), bf16[256,768]{1,0:T(8,128)(2,1)}) %reduce-scatter.17.cloned.1.call-update) | async-done | bytes 393232 | tf_op jit(solution)/shard_map/reduce_scatter | solution.py:297
  387.0 56.8 %all-gather.27.cloned.1.call-done.w_ref = bf16[768,6144]{1,0:T(8,128)(2,1)} async-done(((bf16[96,6144]{1,0:T(8,128)(2,1)}), bf16[768,6144]{1,0:T(8,128)(2,1)}) %all-gather.27.cloned.1.call-update) | async-done | bytes 9437200 | tf_op jit(solution)/shard_map/all_gather | solution.py:341
  443.9 38.7 %all-gather.25.cloned.1.call-done.b_ref = bf16[1024,768]{1,0:T(8,128)(2,1)} async-done(((bf16[256,768]{1,0:T(8,128)(2,1)}), bf16[1024,768]{1,0:T(8,128)(2,1)}) %all-gather.25.cloned.1.call-update) | async-done | bytes 1572880 | tf_op jit(solution)/shard_map/all_gather | solution.py:293
  484.0 11.6 %shard_map.181 = (bf16[1024,768]{1,0:T(8,128)(2,1)}, bf16[1024,768]{1,0:T(8,128)(2,1)S(1)}, f32[1024,768]{1,0:T(8,128)}) custom-call(bf16[1024,768]{1,0:T(8,128)(2,1)S(1)} %copy-done.4, s32[1,1024]{1,0:T(1,128)S(1)} %bitcast.87, s32[1024,1]{1,0:T(8,128)S(1)} %copy.43.col_ref, bf16[768,6144]{1,0:T(8,128)(2,1)} %all-gather.27.cloned.1.call-done.w_ref), custom_call_target="tpu_custom_call" | custom-call | flops 5637144576 | bytes 20971520 | tf_op jit(solution)/shard_map/pallas_call | solution.py:205
  498.2 32.8 %reduce-scatter.19.cloned.1.call-done = bf16[256,768]{1,0:T(8,128)(2,1)} async-done(((bf16[1024,768]{1,0:T(8,128)(2,1)}), bf16[256,768]{1,0:T(8,128)(2,1)}) %reduce-scatter.19.cloned.1.call-update) | async-done | bytes 393232 | tf_op jit(solution)/shard_map/reduce_scatter | solution.py:297
  531.1 2.1 fusion.12
  533.6 35.7 %all-gather.29.cloned.1.call-done.dc_ref = bf16[1024,768]{1,0:T(8,128)(2,1)} async-done(((bf16[256,768]{1,0:T(8,128)(2,1)}), bf16[1024,768]{1,0:T(8,128)(2,1)}) %all-gather.29.cloned.1.call-update) | async-done | bytes 1572880 | tf_op jit(solution)/shard_map/all_gather | solution.py:293
  572.2 15.7 %shard_map.182 = (bf16[1024,768]{1,0:T(8,128)(2,1)}, bf16[768,6144]{1,0:T(8,128)(2,1)}) custom-call(bf16[1024,768]{1,0:T(8,128)(2,1)S(1)} %copy-done.5, s32[1,1024]{1,0:T(1,128)S(1)} %bitcast.88, s32[1024,1]{1,0:T(8,128)S(1)} %copy.43.col_ref, bf16[1024,768]{1,0:T(8,128)(2,1)S(1)} %copy-done.9, f32[1024,768]{1,0:T(8,128)} %get-tuple-element.34.pre_ref, ...), custom_call_target="tpu_custom_call" | custom-call | flops 8053063680 | bytes 31457280 | tf_op jit(solution)/shard_map/pallas_call | solution.py:263
  588.0 34.2 %reduce-scatter.21.cloned.1.call-done = bf16[256,768]{1,0:T(8,128)(2,1)} async-done(((bf16[1024,768]{1,0:T(8,128)(2,1)}), bf16[256,768]{1,0:T(8,128)(2,1)}) %reduce-scatter.21.cloned.1.call-update) | async-done | bytes 393232 | tf_op jit(solution)/shard_map/reduce_scatter | solution.py:297
  622.2 1.9 multiply_reduce_fusion
  624.2 3.0 fusion.35
  627.2 36.2 %all-gather.31.cloned.1.call-done.da_ref = bf16[1024,768]{1,0:T(8,128)(2,1)} async-done(((bf16[256,768]{1,0:T(8,128)(2,1)}), bf16[1024,768]{1,0:T(8,128)(2,1)}) %all-gather.31.cloned.1.call-update) | async-done | bytes 1572880 | tf_op jit(solution)/shard_map/all_gather | solution.py:293
  665.8 23.5 %shard_map.183 = (bf16[1024,768]{1,0:T(8,128)(2,1)}, bf16[768,768]{1,0:T(8,128)(2,1)}) custom-call(bf16[1024,768]{1,0:T(8,128)(2,1)} %all-gather.31.cloned.1.call-done.da_ref, bf16[1024,768]{1,0:T(8,128)(2,1)} %all-gather.23.cloned.1.call-done.a_ref, bf16[1024,576]{1,0:T(8,128)(2,1)S(1)} %copy-done.13, bf16[1024,192]{1,0:T(8,128)(2,1)S(1)} %copy-done.17, ...), custom_call_target="tpu_custom_call" | custom-call | flops 10468982784 | bytes 10485760 | tf_op jit(solution)/shard_map/pallas_call | solution.py:146
  689.6 34.1 %reduce-scatter.23.cloned.1.call-done = bf16[256,768]{1,0:T(8,128)(2,1)} async-done(((bf16[1024,768]{1,0:T(8,128)(2,1)}), bf16[256,768]{1,0:T(8,128)(2,1)}) %reduce-scatter.23.cloned.1.call-update) | async-done | bytes 393232 | tf_op jit(solution)/shard_map/reduce_scatter | solution.py:297
  725.0 1.7 fusion.7
  727.6 36.1 %all-gather.33.cloned.1.call-done.dc_ref = bf16[1024,768]{1,0:T(8,128)(2,1)} async-done(((bf16[256,768]{1,0:T(8,128)(2,1)}), bf16[1024,768]{1,0:T(8,128)(2,1)}) %all-gather.33.cloned.1.call-update) | async-done | bytes 1572880 | tf_op jit(solution)/shard_map/all_gather | solution.py:293
  766.6 15.7 %shard_map.184 = (bf16[1024,768]{1,0:T(8,128)(2,1)}, bf16[768,6144]{1,0:T(8,128)(2,1)}) custom-call(bf16[1024,768]{1,0:T(8,128)(2,1)S(1)} %copy-done.3, s32[1,1024]{1,0:T(1,128)S(1)} %bitcast.89, s32[1024,1]{1,0:T(8,128)S(1)} %copy.43.col_ref, bf16[1024,768]{1,0:T(8,128)(2,1)S(1)} %copy-done.7, f32[1024,768]{1,0:T(8,128)} %get-tuple-element.40.pre_ref, ...), custom_call_target="tpu_custom_call" | custom-call | flops 8053063680 | bytes 31457280 | tf_op jit(solution)/shard_map/pallas_call | solution.py:263
  782.4 34.2 %reduce-scatter.25.cloned.1.call-done = bf16[256,768]{1,0:T(8,128)(2,1)} async-done(((bf16[1024,768]{1,0:T(8,128)(2,1)}), bf16[256,768]{1,0:T(8,128)(2,1)}) %reduce-scatter.25.cloned.1.call-update) | async-done | bytes 393232 | tf_op jit(solution)/shard_map/reduce_scatter | solution.py:297
  816.6 1.7 multiply_reduce_fusion.1
  818.4 1.6 fusion.32
  821.4 34.8 %all-gather.35.cloned.1.call-done.da_ref = bf16[1024,768]{1,0:T(8,128)(2,1)} async-done(((bf16[256,768]{1,0:T(8,128)(2,1)}), bf16[1024,768]{1,0:T(8,128)(2,1)}) %all-gather.35.cloned.1.call-update) | async-done | bytes 1572880 | tf_op jit(solution)/shard_map/all_gather | solution.py:293
  856.2 23.5 %shard_map.185 = (bf16[1024,768]{1,0:T(8,128)(2,1)}, bf16[768,768]{1,0:T(8,128)(2,1)}) custom-call(bf16[1024,768]{1,0:T(8,128)(2,1)} %all-gather.35.cloned.1.call-done.da_ref, bf16[1024,768]{1,0:T(8,128)(2,1)} %all-gather.15.cloned.1.call-done.a_ref, bf16[1024,576]{1,0:T(8,128)(2,1)S(1)} %copy-done.11, bf16[1024,192]{1,0:T(8,128)(2,1)S(1)} %copy-done.15, ...), custom_call_target="tpu_custom_call" | custom-call | flops 10468982784 | bytes 10485760 | tf_op jit(solution)/shard_map/pallas_call | solution.py:146
  882.1 52.8 %reduce-scatter.35.cloned.1.call-done = bf16[96,6144]{1,0:T(8,128)(2,1)} async-done(((bf16[768,6144]{1,0:T(8,128)(2,1)}), bf16[96,6144]{1,0:T(8,128)(2,1)}) %reduce-scatter.35.cloned.1.call-update) | async-done | bytes 1179664 | tf_op jit(solution)/shard_map/reduce_scatter | solution.py:401
  934.9 1.9 stack.38
  937.1 38.5 %reduce-scatter.31.cloned.1.call-done = bf16[96,768]{1,0:T(8,128)(2,1)} async-done(((bf16[768,768]{1,0:T(8,128)(2,1)}), bf16[96,768]{1,0:T(8,128)(2,1)}) %reduce-scatter.31.cloned.1.call-update) | async-done | bytes 147472 | tf_op jit(solution)/shard_map/reduce_scatter | solution.py:400
  975.5 40.3 %reduce-scatter.29.cloned.1.call-done = bf16[96,768]{1,0:T(8,128)(2,1)} async-done(((bf16[768,768]{1,0:T(8,128)(2,1)}), bf16[96,768]{1,0:T(8,128)(2,1)}) %reduce-scatter.29.cloned.1.call-update) | async-done | bytes 147472 | tf_op jit(solution)/shard_map/reduce_scatter | solution.py:400
  1020.0 34.1 %reduce-scatter.27.cloned.1.call-done = bf16[256,768]{1,0:T(8,128)(2,1)} async-done(((bf16[1024,768]{1,0:T(8,128)(2,1)}), bf16[256,768]{1,0:T(8,128)(2,1)}) %reduce-scatter.27.cloned.1.call-update) | async-done | bytes 393232 | tf_op jit(solution)/shard_map/reduce_scatter | solution.py:297
  1055.5 39.8 %psum.7 = f32[12,768]{1,0:T(8,128)S(1)} all-reduce(f32[12,768]{1,0:T(8,128)S(1)} %concatenate.12), channel_id=1, replica_groups=mesh['fsdp'=8,'tp'=4] {'fsdp','tp'}, use_global_device_ids=true, to_apply=%region_30.31 | all-reduce | flops 9216 | bytes 73728 | tf_op jit(solution)/shard_map/psum | solution.py:406
  1096.6 2.1 fusion.15
  1098.7 34.8 %reduce-scatter.33.cloned.1.call-done = bf16[96,6144]{1,0:T(8,128)(2,1)} async-done(((bf16[768,6144]{1,0:T(8,128)(2,1)}), bf16[96,6144]{1,0:T(8,128)(2,1)}) %reduce-scatter.33.cloned.1.call-update) | async-done | bytes 1179664 | tf_op jit(solution)/shard_map/reduce_scatter | solution.py:401
  1133.5 2.8 stack.37
  1138.1 2.6 slice_bitcast_fusion
  (202 shorter events, 58.1 us)
Async XLA Ops:
  7.2 5.8 copy-start.18
  7.2 33.4 %all-gather.13.cloned.1.call-start = ((), (), s32[]{:S(2)}) async-start(), calls=%async_computation.12 | async-start | bytes 1548288 | tf_op jit(solution)/shard_map/all_gather | solution.py:340
  12.9 68.1 %all-gather.15.cloned.1.call-start = ((), (), s32[]{:S(2)}) async-start(), calls=%async_computation.13 | async-start | bytes 1966080 | tf_op jit(solution)/shard_map/all_gather | solution.py:293
  41.6 39.4 %copy-start = (bf16[768,896]{1,0:T(8,128)(2,1)S(1)}, bf16[768,896]{1,0:T(8,128)(2,1)}, u32[]{:S(2)}) copy-start(bf16[768,896]{1,0:T(8,128)(2,1)} %all-gather.13.cloned.1.call-done.w_ref) | copy-start | bytes 4128772
  43.7 86.4 %reduce-scatter.13.cloned.1.call-start = ((), (), s32[]{:S(2)}) async-start(), calls=%async_computation.14 | async-start | bytes 1966080 | tf_op jit(solution)/shard_map/reduce_scatter | solution.py:297
  95.8 37.5 %copy-start.33 = (bf16[2,4,96,768]{3,2,1,0:T(8,128)(2,1)S(1)}, bf16[2,4,96,768]{3,2,1,0:T(8,128)(2,1)}, u32[]{:S(2)}) copy-start(bf16[2,4,96,768]{3,2,1,0:T(8,128)(2,1)} %param.18) | copy-start | bytes 3538948
  95.8 73.7 %all-gather.17.cloned.1.call-start = ((), (), s32[]{:S(2)}) async-start(), calls=%async_computation.15 | async-start | bytes 1966080 | tf_op jit(solution)/shard_map/all_gather | solution.py:293
  133.2 96.2 %all-gather.19.cloned.1.call-start = ((), (), s32[]{:S(2)}) async-start(), calls=%async_computation.16 | async-start | bytes 10616832 | tf_op jit(solution)/shard_map/all_gather | solution.py:341
  138.8 1.8 copy-start.35
  138.8 1.8 copy-start.36
  138.8 117.9 %all-gather.21.cloned.1.call-start = ((), (), s32[]{:S(2)}) async-start(), calls=%async_computation.18 | async-start | bytes 1548288 | tf_op jit(solution)/shard_map/all_gather | solution.py:340
  140.5 154.4 %reduce-scatter.15.cloned.1.call-start = ((), (), s32[]{:S(2)}) async-start(), calls=%async_computation.17 | async-start | bytes 1966080 | tf_op jit(solution)/shard_map/reduce_scatter | solution.py:297
  229.5 1.4 copy-start.2
  243.6 91.0 %all-gather.23.cloned.1.call-start = ((), (), s32[]{:S(2)}) async-start(), calls=%async_computation.19 | async-start | bytes 1966080 | tf_op jit(solution)/shard_map/all_gather | solution.py:293
  243.9 14.9 %copy-start.26 = (bf16[256,768]{1,0:T(8,128)(2,1)S(1)}, bf16[256,768]{1,0:T(8,128)(2,1)}, u32[]{:S(2)}) copy-start(bf16[256,768]{1,0:T(8,128)(2,1)} %multiply_convert_fusion.3) | copy-start | bytes 1179652
  294.9 39.7 %copy-start.1 = (bf16[768,896]{1,0:T(8,128)(2,1)S(1)}, bf16[768,896]{1,0:T(8,128)(2,1)}, u32[]{:S(2)}) copy-start(bf16[768,896]{1,0:T(8,128)(2,1)} %all-gather.21.cloned.1.call-done.w_ref) | copy-start | bytes 4128772
  298.4 85.4 %reduce-scatter.17.cloned.1.call-start = ((), (), s32[]{:S(2)}) async-start(), calls=%async_computation.20 | async-start | bytes 1966080 | tf_op jit(solution)/shard_map/reduce_scatter | solution.py:297
  349.4 94.4 %all-gather.27.cloned.1.call-start = ((), (), s32[]{:S(2)}) async-start(), calls=%async_computation.22 | async-start | bytes 10616832 | tf_op jit(solution)/shard_map/all_gather | solution.py:341
  355.8 126.8 %all-gather.25.cloned.1.call-start = ((), (), s32[]{:S(2)}) async-start(), calls=%async_computation.21 | async-start | bytes 1966080 | tf_op jit(solution)/shard_map/all_gather | solution.py:293
  387.0 144.1 %reduce-scatter.19.cloned.1.call-start = ((), (), s32[]{:S(2)}) async-start(), calls=%async_computation.23 | async-start | bytes 1966080 | tf_op jit(solution)/shard_map/reduce_scatter | solution.py:297
  482.6 1.4 copy-start.4
  496.7 72.6 %all-gather.29.cloned.1.call-start = ((), (), s32[]{:S(2)}) async-start(), calls=%async_computation.24 | async-start | bytes 1966080 | tf_op jit(solution)/shard_map/all_gather | solution.py:293
  533.1 89.1 %reduce-scatter.21.cloned.1.call-start = ((), (), s32[]{:S(2)}) async-start(), calls=%async_computation.25 | async-start | bytes 1966080 | tf_op jit(solution)/shard_map/reduce_scatter | solution.py:297
  569.4 1.4 copy-start.5
  570.8 1.4 copy-start.9
  587.9 75.5 %all-gather.31.cloned.1.call-start = ((), (), s32[]{:S(2)}) async-start(), calls=%async_computation.26 | async-start | bytes 1966080 | tf_op jit(solution)/shard_map/all_gather | solution.py:293
  622.2 2.0 copy-start.24
  622.2 2.0 copy-start.32
  627.2 96.5 %reduce-scatter.23.cloned.1.call-start = ((), (), s32[]{:S(2)}) async-start(), calls=%async_computation.27 | async-start | bytes 1966080 | tf_op jit(solution)/shard_map/reduce_scatter | solution.py:297
  689.3 34.4 %copy-start.22 = (f32[256,768]{1,0:T(8,128)S(1)}, f32[256,768]{1,0:T(8,128)}, u32[]{:S(2)}) copy-start(f32[256,768]{1,0:T(8,128)} %copy-done.21) | copy-start | bytes 2359300
  689.3 74.4 %all-gather.33.cloned.1.call-start = ((), (), s32[]{:S(2)}) async-start(), calls=%async_computation.28 | async-start | bytes 1966080 | tf_op jit(solution)/shard_map/all_gather | solution.py:293
  723.7 1.4 copy-start.30
  727.6 89.1 %reduce-scatter.25.cloned.1.call-start = ((), (), s32[]{:S(2)}) async-start(), calls=%async_computation.29 | async-start | bytes 1966080 | tf_op jit(solution)/shard_map/reduce_scatter | solution.py:297
  763.8 1.4 copy-start.3
  765.2 1.4 copy-start.7
  782.3 34.3 %copy-start.19 = (bf16[256,768]{1,0:T(8,128)(2,1)S(1)}, bf16[256,768]{1,0:T(8,128)(2,1)}, u32[]{:S(2)}) copy-start(bf16[256,768]{1,0:T(8,128)(2,1)} %param.11) | copy-start | bytes 1179652
  782.3 34.3 %copy-start.25 = (bf16[256,768]{1,0:T(8,128)(2,1)S(1)}, bf16[256,768]{1,0:T(8,128)(2,1)}, u32[]{:S(2)}) copy-start(bf16[256,768]{1,0:T(8,128)(2,1)} %reduce-scatter.13.cloned.1.call-done) | copy-start | bytes 1179652
  782.3 73.8 %all-gather.35.cloned.1.call-start = ((), (), s32[]{:S(2)}) async-start(), calls=%async_computation.30 | async-start | bytes 1966080 | tf_op jit(solution)/shard_map/all_gather | solution.py:293
  816.6 1.7 copy-start.31
  820.0 114.9 %reduce-scatter.35.cloned.1.call-start = ((), (), s32[]{:S(2)}) async-start(), calls=%async_computation.35 | async-start | bytes 10616832 | tf_op jit(solution)/shard_map/reduce_scatter | solution.py:401
  820.0 36.2 %copy-start.11 = (bf16[1024,576]{1,0:T(8,128)(2,1)S(1)}, bf16[1024,576]{1,0:T(8,128)(2,1)}, u32[]{:S(2)}) copy-start(bf16[1024,576]{1,0:T(8,128)(2,1)} %copy-done.10) | copy-start | bytes 3538948
  820.0 36.2 %copy-start.15 = (bf16[1024,192]{1,0:T(8,128)(2,1)S(1)}, bf16[1024,192]{1,0:T(8,128)(2,1)}, u32[]{:S(2)}) copy-start(bf16[1024,192]{1,0:T(8,128)(2,1)} %copy-done.14) | copy-start | bytes 1179652
  820.6 155.0 %reduce-scatter.31.cloned.1.call-start = ((), (), s32[]{:S(2)}) async-start(), calls=%async_computation.33 | async-start | bytes 1327104 | tf_op jit(solution)/shard_map/reduce_scatter | solution.py:400
  821.3 194.6 %reduce-scatter.29.cloned.1.call-start = ((), (), s32[]{:S(2)}) async-start(), calls=%async_computation.32 | async-start | bytes 1327104 | tf_op jit(solution)/shard_map/reduce_scatter | solution.py:400
  879.7 174.4 %reduce-scatter.27.cloned.1.call-start = ((), (), s32[]{:S(2)}) async-start(), calls=%async_computation.31 | async-start | bytes 1966080 | tf_op jit(solution)/shard_map/reduce_scatter | solution.py:297
  880.5 253.1 %reduce-scatter.33.cloned.1.call-start = ((), (), s32[]{:S(2)}) async-start(), calls=%async_computation.34 | async-start | bytes 10616832 | tf_op jit(solution)/shard_map/reduce_scatter | solution.py:401
  1018.7 35.4 %copy-start.20 = (bf16[256,768]{1,0:T(8,128)(2,1)S(1)}, bf16[256,768]{1,0:T(8,128)(2,1)}, u32[]{:S(2)}) copy-start(bf16[256,768]{1,0:T(8,128)(2,1)} %param.11) | copy-start | bytes 1179652
  1018.9 77.7 %copy-start.29 = (f32[256,768]{1,0:T(8,128)S(1)}, f32[256,768]{1,0:T(8,128)}, u32[]{:S(2)}) copy-start(f32[256,768]{1,0:T(8,128)} %get-tuple-element.88) | copy-start | bytes 2359300
  (13 other events, 13.8 us)
Sparse Core Ops, SparseCore 0:
  13.0 27.5 all-gather.12
  43.8 37.0 all-gather.14
  95.9 34.1 reduce-scatter.12
  133.3 36.0 all-gather.16
  171.7 57.6 all-gather.18
  231.8 24.8 all-gather.20
  259.6 35.2 reduce-scatter.14
  298.5 36.0 all-gather.22
  349.6 34.1 reduce-scatter.16
  386.1 57.7 all-gather.26
  445.4 37.0 all-gather.24
  496.9 34.1 reduce-scatter.18
  533.3 36.0 all-gather.28
  588.0 34.1 reduce-scatter.20
  627.3 36.0 all-gather.30
  689.5 34.1 reduce-scatter.22
  727.7 36.0 all-gather.32
  782.5 34.1 reduce-scatter.24
  820.1 36.0 all-gather.34
  859.5 75.3 reduce-scatter.34
  938.7 36.7 reduce-scatter.30
  979.1 36.7 reduce-scatter.28
  1018.8 35.2 reduce-scatter.26
  1057.4 76.0 reduce-scatter.32

commit v2 on v1

--- a/solution.py
+++ b/solution.py
@@ -1,3 +1,5 @@
+import functools
+
 import jax
 import jax.numpy as jnp
 from jax import lax
@@ -289,12 +291,199 @@
     )(dc_rows, pos_row, pos_col, buffer, pre, w_pack)
 
 
+MESH = pl.DeviceIdType.MESH
+SUB = 2
+
+
+def greet(me, count):
+    barrier = pltpu.get_barrier_semaphore()
+
+    @pl.when(me > 0)
+    def _():
+        pl.semaphore_signal(barrier, inc=1, device_id={"tp": me - 1}, device_id_type=MESH)
+
+    @pl.when(me < count - 1)
+    def _():
+        pl.semaphore_signal(barrier, inc=1, device_id={"tp": me + 1}, device_id_type=MESH)
+
+    inside = (me > 0) & (me < count - 1)
+
+    @pl.when(inside)
+    def _():
+        pl.semaphore_wait(barrier, 2)
+
+    @pl.when(jnp.logical_not(inside))
+    def _():
+        pl.semaphore_wait(barrier, 1)
+
+
+def gather_body(count, part_ref, out_ref, own_sem, send_sem, recv_sem):
+    me = lax.axis_index("tp")
+    piece = part_ref.shape[0] // SUB
+    own = pltpu.make_async_copy(
+        part_ref, out_ref.at[pl.ds(pl.multiple_of(me * piece * SUB, piece), piece * SUB)], own_sem
+    )
+    own.start()
+    greet(me, count)
+
+    def copy(way, step, sub):
+        sign = 1 - 2 * way
+        chunk = me - sign * step
+        place = pl.ds(pl.multiple_of((chunk * SUB + sub) * piece, piece), piece)
+        source = part_ref.at[pl.ds(sub * piece, piece)] if step == 0 else out_ref.at[place]
+        return pltpu.make_async_remote_copy(
+            src_ref=source,
+            dst_ref=out_ref.at[place],
+            send_sem=send_sem.at[way, step, sub],
+            recv_sem=recv_sem.at[way, step, sub],
+            device_id={"tp": me + sign},
+            device_id_type=MESH,
+        )
+
+    def arrived(way, step, sub):
+        sign = 1 - 2 * way
+        chunk = me - sign * (step + 1)
+        place = pl.ds(pl.multiple_of((chunk * SUB + sub) * piece, piece), piece)
+        pltpu.make_async_remote_copy(
+            src_ref=out_ref.at[place],
+            dst_ref=out_ref.at[place],
+            send_sem=send_sem.at[way, step, sub],
+            recv_sem=recv_sem.at[way, step, sub],
+            device_id={"tp": me - sign},
+            device_id_type=MESH,
+        ).wait_recv()
+
+    def has(way, step):
+        return me >= step if way == 0 else me + step <= count - 1
+
+    def sends(way, step):
+        return has(way, step) & (me < count - 1 if way == 0 else me > 0)
+
+    for step in range(count):
+        for sub in range(SUB):
+            for way in range(2):
+                if step > 0:
+
+                    @pl.when(has(way, step))
+                    def _():
+                        arrived(way, step - 1, sub)
+
+                if step < count - 1:
+
+                    @pl.when(sends(way, step))
+                    def _():
+                        copy(way, step, sub).start()
+
+    for step in range(count - 1):
+        for sub in range(SUB):
+            for way in range(2):
+
+                @pl.when(sends(way, step))
+                def _():
+                    copy(way, step, sub).wait_send()
+
+    own.wait()
+
+
 def gather_tokens(part):
-    return lax.all_gather(part, "tp", axis=0, tiled=True)
+    count = lax.axis_size("tp")
+    tokens, width = part.shape
+    return pl.pallas_call(
+        functools.partial(gather_body, count),
+        in_specs=[pl.BlockSpec(memory_space=pl.ANY)],
+        out_specs=pl.BlockSpec(memory_space=pl.ANY),
+        out_shape=jax.ShapeDtypeStruct((count * tokens, width), part.dtype),
+        scratch_shapes=[
+            pltpu.SemaphoreType.DMA,
+            pltpu.SemaphoreType.DMA((2, count - 1, SUB)),
+            pltpu.SemaphoreType.DMA((2, count - 1, SUB)),
+        ],
+        compiler_params=pltpu.CompilerParams(collective_id=0, has_side_effects=True),
+        cost_estimate=pl.CostEstimate(flops=0, bytes_accessed=80 * 1024 * 1024, transcendentals=0),
+    )(part)
+
+
+def scatter_body(count, whole_ref, out_ref, held_ref, sent_ref, send_sem, recv_sem):
+    me = lax.axis_index("tp")
+    tokens = out_ref.shape[0]
+    piece = tokens // SUB
+    greet(me, count)
+
+    def rows(chunk, sub):
+        return pl.ds(pl.multiple_of(chunk * tokens + sub * piece, piece), piece)
+
+    def copy(way, step, sub):
+        sign = 1 - 2 * way
+        return pltpu.make_async_remote_copy(
+            src_ref=sent_ref.at[way, step, pl.ds(sub * piece, piece)],
+            dst_ref=held_ref.at[way, step, pl.ds(sub * piece, piece)],
+            send_sem=send_sem.at[way, step, sub],
+            recv_sem=recv_sem.at[way, step, sub],
+            device_id={"tp": me + sign},
+            device_id_type=MESH,
+        )
+
+    def goes(way, chunk):
+        return me < chunk if way == 0 else me > chunk
+
+    def first(way):
+        return me == 0 if way == 0 else me == count - 1
+
+    for sub in range(SUB):
+        out_ref[sub * piece : (sub + 1) * piece, :] = whole_ref[rows(me, sub), :].astype(F32)
+    for step in range(count - 1):
+        for sub in range(SUB):
+            for way in range(2):
+                chunk = count - 1 - step if way == 0 else step
+                part = pl.ds(sub * piece, piece)
+
+                @pl.when(goes(way, chunk) & first(way))
+                def _():
+                    sent_ref[way, step, part, :] = whole_ref[rows(chunk, sub), :]
+                    copy(way, step, sub).start()
+
+                @pl.when(goes(way, chunk) & jnp.logical_not(first(way)))
+                def _():
+                    copy(way, step, sub).wait_recv()
+                    total = whole_ref[rows(chunk, sub), :].astype(F32)
+                    total = total + held_ref[way, step, part, :].astype(F32)
+                    sent_ref[way, step, part, :] = total.astype(BF)
+                    copy(way, step, sub).start()
+
+                @pl.when((me == chunk) & jnp.logical_not(first(way)))
+                def _():
+                    copy(way, step, sub).wait_recv()
+                    out_ref[part, :] += held_ref[way, step, part, :].astype(F32)
+
+    for step in range(count - 1):
+        for sub in range(SUB):
+            for way in range(2):
+                chunk = count - 1 - step if way == 0 else step
+
+                @pl.when(goes(way, chunk))
+                def _():
+                    copy(way, step, sub).wait_send()
 
 
 def scatter_tokens(whole):
-    return lax.psum_scatter(whole, "tp", scatter_dimension=0, tiled=True).astype(F32)
+    count = lax.axis_size("tp")
+    tokens, width = whole.shape[0] // count, whole.shape[1]
+    return pl.pallas_call(
+        functools.partial(scatter_body, count),
+        in_specs=[pl.BlockSpec(memory_space=pltpu.VMEM)],
+        out_specs=pl.BlockSpec(memory_space=pltpu.VMEM),
+        out_shape=jax.ShapeDtypeStruct((tokens, width), F32),
+        scratch_shapes=[
+            pltpu.VMEM((2, count - 1, tokens, width), BF),
+            pltpu.VMEM((2, count - 1, tokens, width), BF),
+            pltpu.SemaphoreType.DMA((2, count - 1, SUB)),
+            pltpu.SemaphoreType.DMA((2, count - 1, SUB)),
+        ],
+        compiler_params=pltpu.CompilerParams(
+            collective_id=1, has_side_effects=True, vmem_limit_bytes=24 * 1024 * 1024
+        ),
+        cost_estimate=pl.CostEstimate(flops=0, bytes_accessed=80 * 1024 * 1024, transcendentals=0),
+    )(whole)
 
 
 def local(

time: 1160 us -> 1180 us (1.017)
  Pallas kernels: 127 us -> 954 us
  waiting for transfers between devices: 877 us -> 83.8 us
  blocking collectives: 39.8 us -> 54 us
    pallas_call x0 -> x16, Pallas kernels: none -> 831 us  [the longest x8 556 us: scatter_tokens(): pl.pallas_call(functools.partial(scatter_body, count), in_specs=[pl.Block...]
    all_gather x8 -> x0, waiting for transfers between devices: 284 us -> none  [gather_tokens(): return lax.all_gather(part, 'tp', axis=0, tiled=True)]
    reduce_scatter x8 -> x0, waiting for transfers between devices: 267 us -> none  [scatter_tokens(): lax.psum_scatter(whole, 'tp', scatter_dimension=0, tiled=True).astype(F32)]
    all_gather x2, waiting for transfers between devices: 117 us -> 0.04 us  [local(): lax.all_gather(large, 'fsdp', axis=0, tiled=True)]
    reduce_scatter x2, waiting for transfers between devices: 78.8 us -> 0.01 us  [local(): lax.psum_scatter(grad_attn, 'fsdp', scatter_dimension=0, tiled=True)]
    all_gather x2, waiting for transfers between devices: 40.3 us -> 17.4 us  [local(): lax.all_gather(jnp.concatenate(small, 1), 'fsdp', axis=0, tiled=True)]
    reduce_scatter x2, waiting for transfers between devices: 87.6 us -> 64.9 us  [local(): lax.psum_scatter(grad_experts, 'fsdp', scatter_dimension=0, tiled=True)]
    psum x1, blocking collectives: 39.8 us -> 54 us  [local(): sums = lax.psum(jnp.concatenate(small_sums, 0), ('fsdp', 'tp'))]
  transfers between devices with their start and end apart: 24 -> 8, of which waited for: 24 -> 2; matrix products, arithmetic and copies ran while one was open for 3% -> 3% of each run, Pallas kernels for 3% -> 53%
where the time goes in v2:
time: 1180 us; the launch traced here: 1170 us
  Pallas kernels  954 us (81%)
  waiting for transfers between devices  83.8 us (7%)
  blocking collectives  54 us (5%)
  local copies, waits for them, and re-layouts  42.7 us (4%)
  other arithmetic  23.1 us (2%)
  between operations  15.8 us (1%)
    pallas_call x8, Pallas kernels, scatter_tokens(): pl.pallas_call(functools.partial(scatter_body, count), in_specs=[pl.Block...  556 us
    pallas_call x8, Pallas kernels, gather_tokens(): pl.pallas_call(functools.partial(gather_body, count), in_specs=[pl.BlockS...  275 us
    reduce_scatter x2, waiting for transfers between devices, local(): lax.psum_scatter(grad_experts, 'fsdp', scatter_dimension=0, tiled=True)  64.9 us
    psum x1, blocking collectives, local(): sums = lax.psum(jnp.concatenate(small_sums, 0), ('fsdp', 'tp'))  54 us
    pallas_call x2, Pallas kernels, attend_behind(): pl.pallas_call(attend_behind_body, grid=(tokens // BLOCK,), in_specs=[who...  45.9 us
    pallas_call x2, Pallas kernels, experts_behind(): pl.pallas_call(experts_behind_body, grid=(experts,), in_specs=[whole_spec...  30.4 us
    pallas_call x2, Pallas kernels, attend_ahead(): pl.pallas_call(attend_ahead_body, grid=(tokens // BLOCK,), in_specs=[whol...  24.2 us
  transfers between devices with their start and end apart: 8, of which 2 were waited for; matrix products, arithmetic and copies ran while one was open for 3% of the time, Pallas kernels for 53%

profile of v2, /device:TPU:0, one launch (start us, length us, event | category | flops | bytes accessed | tf_op | source)
XLA Modules:
  0.0 1174.6 jit_solution(14520681280911063262)
XLA Ops:
  16.1 1.2 copy.42
  17.3 1.7 reshape.145
  19.1 1.2 copy.50
  20.3 1.7 reshape.147
  23.2 17.4 %all-gather.5.cloned.1.call-done.w_ref = bf16[768,896]{1,0:T(8,128)(2,1)} async-done(((bf16[96,896]{1,0:T(8,128)(2,1)}), bf16[768,896]{1,0:T(8,128)(2,1)}) %all-gather.5.cloned.1.call-update) | async-done | bytes 1376272 | tf_op jit(solution)/shard_map/all_gather | solution.py:529
  41.6 1.2 slice_reduce_fusion.3
  43.7 29.7 %shard_map.178.a_ref = bf16[1024,768]{1,0:T(8,128)(2,1)} custom-call(bf16[256,768]{1,0:T(8,128)(2,1)} %fusion.2.part_ref), custom_call_target="tpu_custom_call" | custom-call | bytes 83886080 | tf_op jit(solution)/shard_map/pallas_call | solution.py:391
  73.4 12.1 %shard_map.179 = (bf16[1024,768]{1,0:T(8,128)(2,1)S(1)}, bf16[1024,576]{1,0:T(8,128)(2,1)S(1)}, bf16[1024,192]{1,0:T(8,128)(2,1)S(1)}) custom-call(bf16[1024,768]{1,0:T(8,128)(2,1)} %shard_map.178.a_ref, bf16[768,896]{1,0:T(8,128)(2,1)S(1)} %copy-done.4), custom_call_target="tpu_custom_call" | custom-call | flops 4429185024 | bytes 8388608 | tf_op jit(solution)/shard_map/pallas_call | solution.py:78
  86.6 69.6 %shard_map.180 = f32[256,768]{1,0:T(8,128)S(1)} custom-call(bf16[1024,768]{1,0:T(8,128)(2,1)S(1)} %get-tuple-element.29.whole_ref), custom_call_target="tpu_custom_call" | custom-call | bytes 83886080 | tf_op jit(solution)/shard_map/pallas_call | solution.py:471
  157.5 36.0 %shard_map.181.b_ref = bf16[1024,768]{1,0:T(8,128)(2,1)} custom-call(bf16[256,768]{1,0:T(8,128)(2,1)} %multiply_convert_fusion.3.part_ref), custom_call_target="tpu_custom_call" | custom-call | bytes 83886080 | tf_op jit(solution)/shard_map/pallas_call | solution.py:391
  195.1 1.2 slice_reduce_fusion.7
  196.4 11.0 shard_map.182
  207.4 71.5 %shard_map.183 = f32[256,768]{1,0:T(8,128)S(1)} custom-call(bf16[1024,768]{1,0:T(8,128)(2,1)S(1)} %get-tuple-element.30.whole_ref), custom_call_target="tpu_custom_call" | custom-call | bytes 83886080 | tf_op jit(solution)/shard_map/pallas_call | solution.py:471
  279.9 2.1 multiply_convert_fusion.2.part_ref
  282.1 32.4 %shard_map.184.a_ref = bf16[1024,768]{1,0:T(8,128)(2,1)} custom-call(bf16[256,768]{1,0:T(8,128)(2,1)} %multiply_convert_fusion.2.part_ref), custom_call_target="tpu_custom_call" | custom-call | bytes 83886080 | tf_op jit(solution)/shard_map/pallas_call | solution.py:391
  314.5 12.1 %shard_map.185 = (bf16[1024,768]{1,0:T(8,128)(2,1)S(1)}, bf16[1024,576]{1,0:T(8,128)(2,1)S(1)}, bf16[1024,192]{1,0:T(8,128)(2,1)S(1)}) custom-call(bf16[1024,768]{1,0:T(8,128)(2,1)} %shard_map.184.a_ref, bf16[768,896]{1,0:T(8,128)(2,1)S(1)} %copy-done.6), custom_call_target="tpu_custom_call" | custom-call | flops 4429185024 | bytes 8388608 | tf_op jit(solution)/shard_map/pallas_call | solution.py:78
  327.7 70.0 %shard_map.186 = f32[256,768]{1,0:T(8,128)S(1)} custom-call(bf16[1024,768]{1,0:T(8,128)(2,1)S(1)} %get-tuple-element.31.whole_ref), custom_call_target="tpu_custom_call" | custom-call | bytes 83886080 | tf_op jit(solution)/shard_map/pallas_call | solution.py:471
  397.7 1.3 multiply_reduce_fusion.7
  400.8 34.2 %shard_map.187.b_ref = bf16[1024,768]{1,0:T(8,128)(2,1)} custom-call(bf16[256,768]{1,0:T(8,128)(2,1)} %multiply_convert_fusion.1.part_ref), custom_call_target="tpu_custom_call" | custom-call | bytes 83886080 | tf_op jit(solution)/shard_map/pallas_call | solution.py:391
  435.5 1.4 copy-done.1
  436.9 11.1 shard_map.188
  448.0 72.6 %shard_map.189 = f32[256,768]{1,0:T(8,128)S(1)} custom-call(bf16[1024,768]{1,0:T(8,128)(2,1)S(1)} %get-tuple-element.32.whole_ref), custom_call_target="tpu_custom_call" | custom-call | bytes 83886080 | tf_op jit(solution)/shard_map/pallas_call | solution.py:471
  521.6 34.1 %shard_map.190.dc_ref = bf16[1024,768]{1,0:T(8,128)(2,1)} custom-call(bf16[256,768]{1,0:T(8,128)(2,1)} %get-tuple-element.109.part_ref), custom_call_target="tpu_custom_call" | custom-call | bytes 83886080 | tf_op jit(solution)/shard_map/pallas_call | solution.py:391
  555.8 1.4 copy-done.3
  557.2 1.4 copy-done.11
  558.6 15.2 %shard_map.191 = (bf16[1024,768]{1,0:T(8,128)(2,1)S(1)}, bf16[768,6144]{1,0:T(8,128)(2,1)}) custom-call(bf16[1024,768]{1,0:T(8,128)(2,1)S(1)} %copy-done.3, s32[1,1024]{1,0:T(1,128)S(1)} %bitcast.88, s32[1024,1]{1,0:T(8,128)S(1)} %copy.43.col_ref, bf16[1024,768]{1,0:T(8,128)(2,1)S(1)} %copy-done.11, f32[1024,768]{1,0:T(8,128)} %get-tuple-element.34.pre_ref, ...), custom_call_target="tpu_custom_call" | custom-call | flops 8053063680 | bytes 31457280 | tf_op jit(solution)/shard_map/pallas_call | solution.py:265
  573.7 67.4 %shard_map.192 = f32[256,768]{1,0:T(8,128)S(1)} custom-call(bf16[1024,768]{1,0:T(8,128)(2,1)S(1)} %get-tuple-element.35.whole_ref), custom_call_target="tpu_custom_call" | custom-call | bytes 83886080 | tf_op jit(solution)/shard_map/pallas_call | solution.py:471
  642.4 1.6 fusion.25
  643.9 36.8 %shard_map.193.da_ref = bf16[1024,768]{1,0:T(8,128)(2,1)} custom-call(bf16[256,768]{1,0:T(8,128)(2,1)} %get-tuple-element.107.part_ref), custom_call_target="tpu_custom_call" | custom-call | bytes 83886080 | tf_op jit(solution)/shard_map/pallas_call | solution.py:391
  680.8 1.3 copy-done.15
  683.1 23.0 %shard_map.194 = (bf16[1024,768]{1,0:T(8,128)(2,1)S(1)}, bf16[768,768]{1,0:T(8,128)(2,1)}) custom-call(bf16[1024,768]{1,0:T(8,128)(2,1)} %shard_map.193.da_ref, bf16[1024,768]{1,0:T(8,128)(2,1)} %shard_map.184.a_ref, bf16[1024,576]{1,0:T(8,128)(2,1)S(1)} %copy-done.15, bf16[1024,192]{1,0:T(8,128)(2,1)S(1)} %copy-done.19, bf16[768,896]{1,0:T(8,128)(2,1)S(1)} %copy-done.7), custom_call_target="tpu_custom_call" | custom-call | flops 10468982784 | bytes 10485760 | tf_op jit(solution)/shard_map/pallas_call | solution.py:148
  706.1 72.5 %shard_map.195 = f32[256,768]{1,0:T(8,128)S(1)} custom-call(bf16[1024,768]{1,0:T(8,128)(2,1)S(1)} %get-tuple-element.38.whole_ref), custom_call_target="tpu_custom_call" | custom-call | bytes 83886080 | tf_op jit(solution)/shard_map/pallas_call | solution.py:471
  778.8 1.4 multiply_reduce_fusion.1
  780.3 2.6 multiply_convert_fusion
  783.8 38.0 %shard_map.196.dc_ref = bf16[1024,768]{1,0:T(8,128)(2,1)} custom-call(bf16[256,768]{1,0:T(8,128)(2,1)} %get-tuple-element.89.part_ref), custom_call_target="tpu_custom_call" | custom-call | bytes 83886080 | tf_op jit(solution)/shard_map/pallas_call | solution.py:391
  821.9 1.4 copy-done.2
  823.3 15.3 %shard_map.197 = (bf16[1024,768]{1,0:T(8,128)(2,1)S(1)}, bf16[768,6144]{1,0:T(8,128)(2,1)}) custom-call(bf16[1024,768]{1,0:T(8,128)(2,1)S(1)} %copy-done.2, s32[1,1024]{1,0:T(1,128)S(1)} %bitcast.89, s32[1024,1]{1,0:T(8,128)S(1)} %copy.43.col_ref, bf16[1024,768]{1,0:T(8,128)(2,1)S(1)} %copy-done.9, f32[1024,768]{1,0:T(8,128)} %get-tuple-element.40.pre_ref, ...), custom_call_target="tpu_custom_call" | custom-call | flops 8053063680 | bytes 31457280 | tf_op jit(solution)/shard_map/pallas_call | solution.py:265
  838.6 66.3 %shard_map.198 = f32[256,768]{1,0:T(8,128)S(1)} custom-call(bf16[1024,768]{1,0:T(8,128)(2,1)S(1)} %get-tuple-element.41.whole_ref), custom_call_target="tpu_custom_call" | custom-call | bytes 83886080 | tf_op jit(solution)/shard_map/pallas_call | solution.py:471
  906.0 1.5 fusion.26
  907.5 33.4 %shard_map.199.da_ref = bf16[1024,768]{1,0:T(8,128)(2,1)} custom-call(bf16[256,768]{1,0:T(8,128)(2,1)} %get-tuple-element.87.part_ref), custom_call_target="tpu_custom_call" | custom-call | bytes 83886080 | tf_op jit(solution)/shard_map/pallas_call | solution.py:391
  941.0 1.3 copy-done.13
  942.3 23.0 %shard_map.200 = (bf16[1024,768]{1,0:T(8,128)(2,1)S(1)}, bf16[768,768]{1,0:T(8,128)(2,1)}) custom-call(bf16[1024,768]{1,0:T(8,128)(2,1)} %shard_map.199.da_ref, bf16[1024,768]{1,0:T(8,128)(2,1)} %shard_map.178.a_ref, bf16[1024,576]{1,0:T(8,128)(2,1)S(1)} %copy-done.13, bf16[1024,192]{1,0:T(8,128)(2,1)S(1)} %copy-done.17, bf16[768,896]{1,0:T(8,128)(2,1)S(1)} %copy-done.5), custom_call_target="tpu_custom_call" | custom-call | flops 10468982784 | bytes 10485760 | tf_op jit(solution)/shard_map/pallas_call | solution.py:148
  966.8 66.3 %shard_map.201 = f32[256,768]{1,0:T(8,128)S(1)} custom-call(bf16[1024,768]{1,0:T(8,128)(2,1)S(1)} %get-tuple-element.44.whole_ref), custom_call_target="tpu_custom_call" | custom-call | bytes 83886080 | tf_op jit(solution)/shard_map/pallas_call | solution.py:471
  1034.5 54.0 %psum.7 = f32[12,768]{1,0:T(8,128)S(1)} all-reduce(f32[12,768]{1,0:T(8,128)S(1)} %concatenate.12), channel_id=1, replica_groups=mesh['fsdp'=8,'tp'=4] {'fsdp','tp'}, use_global_device_ids=true, to_apply=%region_22.23 | all-reduce | flops 9216 | bytes 73728 | tf_op jit(solution)/shard_map/psum | solution.py:595
  1095.0 2.0 stack.38
  1097.3 64.9 %reduce-scatter.9.cloned.1.call-done = bf16[96,6144]{1,0:T(8,128)(2,1)} async-done(((bf16[768,6144]{1,0:T(8,128)(2,1)}), bf16[96,6144]{1,0:T(8,128)(2,1)}) %reduce-scatter.9.cloned.1.call-update) | async-done | bytes 1179664 | tf_op jit(solution)/shard_map/reduce_scatter | solution.py:590
  1162.2 1.9 stack.37
  1164.7 2.6 slice_bitcast_fusion
  (222 shorter events, 35.4 us)
Async XLA Ops:
  7.2 33.4 %all-gather.5.cloned.1.call-start = ((), (), s32[]{:S(2)}) async-start(), calls=%async_computation.4 | async-start | bytes 1548288 | tf_op jit(solution)/shard_map/all_gather | solution.py:529
  11.7 2.9 copy-start.37
  12.9 181.1 %all-gather.9.cloned.1.call-start = ((), (), s32[]{:S(2)}) async-start(), calls=%async_computation.6 | async-start | bytes 1548288 | tf_op jit(solution)/shard_map/all_gather | solution.py:529
  14.6 181.8 %all-gather.7.cloned.1.call-start = ((), (), s32[]{:S(2)}) async-start(), calls=%async_computation.5 | async-start | bytes 10616832 | tf_op jit(solution)/shard_map/all_gather | solution.py:530
  19.0 416.4 %all-gather.11.cloned.1.call-start = ((), (), s32[]{:S(2)}) async-start(), calls=%async_computation.7 | async-start | bytes 10616832 | tf_op jit(solution)/shard_map/all_gather | solution.py:530
  20.3 1.8 copy-start.61
  20.3 1.9 copy-start.62
  22.1 1068.8 %reduce-scatter.7.cloned.1.call-start = ((), (), s32[]{:S(2)}) async-start(), calls=%async_computation.9 | async-start | bytes 1327104 | tf_op jit(solution)/shard_map/reduce_scatter | solution.py:589
  23.2 19.6 %copy-start.55 = (f32[256]{0:T(256)}, f32[256]{0:T(256)S(1)}, u32[]{:S(2)}) copy-start(f32[256]{0:T(256)S(1)} %fusion.9) | copy-start | bytes 3076
  42.8 30.6 %copy-start.4 = (bf16[768,896]{1,0:T(8,128)(2,1)S(1)}, bf16[768,896]{1,0:T(8,128)(2,1)}, u32[]{:S(2)}) copy-start(bf16[768,896]{1,0:T(8,128)(2,1)} %all-gather.5.cloned.1.call-done.w_ref) | copy-start | bytes 4128772
  86.6 69.9 %copy-start.16 = (bf16[1024,192]{1,0:T(8,128)(2,1)}, bf16[1024,192]{1,0:T(8,128)(2,1)S(1)}, u32[]{:S(2)}) copy-start(bf16[1024,192]{1,0:T(8,128)(2,1)S(1)} %get-tuple-element.43.mixed_ref) | copy-start | bytes 1179652
  86.6 69.7 %copy-start.26 = (bf16[256,768]{1,0:T(8,128)(2,1)S(1)}, bf16[256,768]{1,0:T(8,128)(2,1)}, u32[]{:S(2)}) copy-start(bf16[256,768]{1,0:T(8,128)(2,1)} %param.11) | copy-start | bytes 1179652
  156.4 37.1 %copy-start.53 = (f32[256]{0:T(256)}, f32[256]{0:T(256)S(1)}, u32[]{:S(2)}) copy-start(f32[256]{0:T(256)S(1)} %get-tuple-element.99) | copy-start | bytes 3076
  156.4 122.4 %copy-start.20 = (f32[256,768]{1,0:T(8,128)}, f32[256,768]{1,0:T(8,128)S(1)}, u32[]{:S(2)}) copy-start(f32[256,768]{1,0:T(8,128)S(1)} %get-tuple-element.100) | copy-start | bytes 2359300
  156.5 37.1 %copy-start.39 = (f32[256]{0:T(256)}, f32[256]{0:T(256)S(1)}, u32[]{:S(2)}) copy-start(f32[256]{0:T(256)S(1)} %fusion.22) | copy-start | bytes 3076
  157.5 36.0 %copy-start.30 = (bf16[256,768]{1,0:T(8,128)(2,1)S(1)}, bf16[256,768]{1,0:T(8,128)(2,1)}, u32[]{:S(2)}) copy-start(bf16[256,768]{1,0:T(8,128)(2,1)} %multiply_convert_fusion.3.part_ref) | copy-start | bytes 1179652
  194.0 2.4 copy-start
  196.3 82.5 %copy-start.41 = (f32[256]{0:T(256)}, f32[256]{0:T(256)S(1)}, u32[]{:S(2)}) copy-start(f32[256]{0:T(256)S(1)} %get-tuple-element.97) | copy-start | bytes 3076
  207.4 72.5 %copy-start.8 = (bf16[1024,768]{1,0:T(8,128)(2,1)}, bf16[1024,768]{1,0:T(8,128)(2,1)S(1)}, u32[]{:S(2)}) copy-start(bf16[1024,768]{1,0:T(8,128)(2,1)S(1)} %get-tuple-element.39.buffer_ref) | copy-start | bytes 4718596
  279.9 34.6 %copy-start.57 = (f32[256]{0:T(256)}, f32[256]{0:T(256)S(1)}, u32[]{:S(2)}) copy-start(f32[256]{0:T(256)S(1)} %get-tuple-element.95) | copy-start | bytes 3076
  279.9 34.6 %copy-start.43 = (f32[256]{0:T(256)}, f32[256]{0:T(256)S(1)}, u32[]{:S(2)}) copy-start(f32[256]{0:T(256)S(1)} %fusion.23) | copy-start | bytes 3076
  279.9 34.6 %copy-start.6 = (bf16[768,896]{1,0:T(8,128)(2,1)S(1)}, bf16[768,896]{1,0:T(8,128)(2,1)}, u32[]{:S(2)}) copy-start(bf16[768,896]{1,0:T(8,128)(2,1)} %all-gather.9.cloned.1.call-done.w_ref) | copy-start | bytes 4128772
  327.7 71.3 %copy-start.18 = (bf16[1024,192]{1,0:T(8,128)(2,1)}, bf16[1024,192]{1,0:T(8,128)(2,1)S(1)}, u32[]{:S(2)}) copy-start(bf16[1024,192]{1,0:T(8,128)(2,1)S(1)} %get-tuple-element.37.mixed_ref) | copy-start | bytes 1179652
  400.8 34.2 %copy-start.32 = (bf16[256,768]{1,0:T(8,128)(2,1)S(1)}, bf16[256,768]{1,0:T(8,128)(2,1)}, u32[]{:S(2)}) copy-start(bf16[256,768]{1,0:T(8,128)(2,1)} %multiply_convert_fusion.1.part_ref) | copy-start | bytes 1179652
  448.0 73.6 %copy-start.10 = (bf16[1024,768]{1,0:T(8,128)(2,1)}, bf16[1024,768]{1,0:T(8,128)(2,1)S(1)}, u32[]{:S(2)}) copy-start(bf16[1024,768]{1,0:T(8,128)(2,1)S(1)} %get-tuple-element.33.buffer_ref) | copy-start | bytes 4718596
  448.0 72.6 %copy-start.34 = (bf16[256,768]{1,0:T(8,128)(2,1)S(1)}, bf16[256,768]{1,0:T(8,128)(2,1)}, u32[]{:S(2)}) copy-start(bf16[256,768]{1,0:T(8,128)(2,1)} %param.12) | copy-start | bytes 1179652
  521.6 120.2 %copy-start.45 = (f32[256,1]{0,1:T(1,128)}, f32[256,1]{0,1:T(1,128)S(1)}, u32[]{:S(2)}) copy-start(f32[256,1]{0,1:T(1,128)S(1)} %get-tuple-element.121) | copy-start | bytes 3076
  521.6 120.2 %copy-start.47 = (f32[256,1]{0,1:T(1,128)}, f32[256,1]{0,1:T(1,128)S(1)}, u32[]{:S(2)}) copy-start(f32[256,1]{0,1:T(1,128)S(1)} %get-tuple-element.122) | copy-start | bytes 3076
  521.6 120.2 %copy-start.49 = (f32[256,1]{0,1:T(1,128)}, f32[256,1]{0,1:T(1,128)S(1)}, u32[]{:S(2)}) copy-start(f32[256,1]{0,1:T(1,128)S(1)} %get-tuple-element.123) | copy-start | bytes 3076
  521.6 120.2 %copy-start.51 = (f32[256,1]{0,1:T(1,128)}, f32[256,1]{0,1:T(1,128)S(1)}, u32[]{:S(2)}) copy-start(f32[256,1]{0,1:T(1,128)S(1)} %get-tuple-element.124) | copy-start | bytes 3076
  573.7 67.4 %copy-start.23 = (f32[256,768]{1,0:T(8,128)S(1)}, f32[256,768]{1,0:T(8,128)}, u32[]{:S(2)}) copy-start(f32[256,768]{1,0:T(8,128)} %copy-done.22) | copy-start | bytes 2359300
  643.9 36.8 %copy-start.7 = (bf16[768,896]{1,0:T(8,128)(2,1)S(1)}, bf16[768,896]{1,0:T(8,128)(2,1)}, u32[]{:S(2)}) copy-start(bf16[768,896]{1,0:T(8,128)(2,1)} %all-gather.9.cloned.1.call-done.w_ref) | copy-start | bytes 4128772
  706.1 72.7 %copy-start.44 = (f32[256]{0:T(256)S(1)}, f32[256]{0:T(256)}, u32[]{:S(2)}) copy-start(f32[256]{0:T(256)} %copy-done.43) | copy-start | bytes 3076
  778.6 1.6 copy-start.35
  778.6 1.6 copy-start.42
  778.7 1.6 copy-start.46
  778.7 312.1 %reduce-scatter.5.cloned.1.call-start = ((), (), s32[]{:S(2)}) async-start(), calls=%async_computation.8 | async-start | bytes 1327104 | tf_op jit(solution)/shard_map/reduce_scatter | solution.py:589
  783.8 38.1 %copy-start.9 = (bf16[1024,768]{1,0:T(8,128)(2,1)S(1)}, bf16[1024,768]{1,0:T(8,128)(2,1)}, u32[]{:S(2)}) copy-start(bf16[1024,768]{1,0:T(8,128)(2,1)} %copy-done.8) | copy-start | bytes 4718596
  838.5 66.3 %copy-start.21 = (f32[256,768]{1,0:T(8,128)S(1)}, f32[256,768]{1,0:T(8,128)}, u32[]{:S(2)}) copy-start(f32[256,768]{1,0:T(8,128)} %copy-done.20) | copy-start | bytes 2359300
  838.6 66.3 %copy-start.40 = (f32[256]{0:T(256)S(1)}, f32[256]{0:T(256)}, u32[]{:S(2)}) copy-start(f32[256]{0:T(256)} %copy-done.39) | copy-start | bytes 3076
  907.5 33.4 %copy-start.5 = (bf16[768,896]{1,0:T(8,128)(2,1)S(1)}, bf16[768,896]{1,0:T(8,128)(2,1)}, u32[]{:S(2)}) copy-start(bf16[768,896]{1,0:T(8,128)(2,1)} %all-gather.5.cloned.1.call-done.w_ref) | copy-start | bytes 4128772
  907.5 33.5 %copy-start.17 = (bf16[1024,192]{1,0:T(8,128)(2,1)S(1)}, bf16[1024,192]{1,0:T(8,128)(2,1)}, u32[]{:S(2)}) copy-start(bf16[1024,192]{1,0:T(8,128)(2,1)} %copy-done.16) | copy-start | bytes 1179652
  965.3 129.8 %reduce-scatter.11.cloned.1.call-start = ((), (), s32[]{:S(2)}) async-start(), calls=%async_computation.11 | async-start | bytes 10616832 | tf_op jit(solution)/shard_map/reduce_scatter | solution.py:590
  966.0 196.2 %reduce-scatter.9.cloned.1.call-start = ((), (), s32[]{:S(2)}) async-start(), calls=%async_computation.10 | async-start | bytes 10616832 | tf_op jit(solution)/shard_map/reduce_scatter | solution.py:590
  966.8 66.4 %copy-start.27 = (bf16[256,768]{1,0:T(8,128)(2,1)S(1)}, bf16[256,768]{1,0:T(8,128)(2,1)}, u32[]{:S(2)}) copy-start(bf16[256,768]{1,0:T(8,128)(2,1)} %param.11) | copy-start | bytes 1179652
  966.8 66.6 %copy-start.33 = (bf16[256,768]{1,0:T(8,128)(2,1)S(1)}, bf16[256,768]{1,0:T(8,128)(2,1)}, u32[]{:S(2)}) copy-start(bf16[256,768]{1,0:T(8,128)(2,1)} %multiply_convert_fusion.1.part_ref) | copy-start | bytes 1179652
  1033.1 55.4 %copy-start.56 = (f32[256]{0:T(256)S(1)}, f32[256]{0:T(256)}, u32[]{:S(2)}) copy-start(f32[256]{0:T(256)} %copy-done.55) | copy-start | bytes 3076
  1033.1 56.6 %copy-start.36 = (f32[256,768]{1,0:T(8,128)S(1)}, f32[256,768]{1,0:T(8,128)}, u32[]{:S(2)}) copy-start(f32[256,768]{1,0:T(8,128)} %get-tuple-element.88) | copy-start | bytes 2359300
  (23 other events, 28.4 us)
Sparse Core Ops, SparseCore 0:
  13.0 27.5 all-gather.4
  43.1 24.8 all-gather.8
  70.4 58.8 all-gather.6
  131.0 58.8 all-gather.10
  778.9 50.1 reduce-scatter.6
  965.4 36.1 reduce-scatter.4
  1005.1 77.0 reduce-scatter.10
  1085.7 76.4 reduce-scatter.8

commit v3 on v2

--- a/solution.py
+++ b/solution.py
@@ -423,26 +423,25 @@
             device_id_type=MESH,
         )
 
-    def goes(way, chunk):
-        return me < chunk if way == 0 else me > chunk
-
     def first(way):
         return me == 0 if way == 0 else me == count - 1
 
     for sub in range(SUB):
         out_ref[sub * piece : (sub + 1) * piece, :] = whole_ref[rows(me, sub), :].astype(F32)
-    for step in range(count - 1):
+    for turn in range(2 * count - 2):
         for sub in range(SUB):
             for way in range(2):
+                step = turn - (me if way == 0 else count - 1 - me)
                 chunk = count - 1 - step if way == 0 else step
                 part = pl.ds(sub * piece, piece)
-
-                @pl.when(goes(way, chunk) & first(way))
+                goes = (step >= 0) & (me < chunk if way == 0 else me > chunk)
+
+                @pl.when(goes & first(way))
                 def _():
                     sent_ref[way, step, part, :] = whole_ref[rows(chunk, sub), :]
                     copy(way, step, sub).start()
 
-                @pl.when(goes(way, chunk) & jnp.logical_not(first(way)))
+                @pl.when(goes & jnp.logical_not(first(way)))
                 def _():
                     copy(way, step, sub).wait_recv()
                     total = whole_ref[rows(chunk, sub), :].astype(F32)
@@ -450,17 +449,22 @@
                     sent_ref[way, step, part, :] = total.astype(BF)
                     copy(way, step, sub).start()
 
-                @pl.when((me == chunk) & jnp.logical_not(first(way)))
-                def _():
-                    copy(way, step, sub).wait_recv()
-                    out_ref[part, :] += held_ref[way, step, part, :].astype(F32)
+    for sub in range(SUB):
+        for way in range(2):
+            step = count - 1 - me if way == 0 else me
+            part = pl.ds(sub * piece, piece)
+
+            @pl.when(jnp.logical_not(first(way)))
+            def _():
+                copy(way, step, sub).wait_recv()
+                out_ref[part, :] += held_ref[way, step, part, :].astype(F32)
 
     for step in range(count - 1):
         for sub in range(SUB):
             for way in range(2):
                 chunk = count - 1 - step if way == 0 else step
 
-                @pl.when(goes(way, chunk))
+                @pl.when(me < chunk if way == 0 else me > chunk)
                 def _():
                     copy(way, step, sub).wait_send()
 
@@ -542,8 +546,10 @@
         rest = w_attn[:, 4 * heads_dim : 4 * heads_dim + 2 + experts]
         rest_rows = rest.astype(F32).T
         gain_one, gain_two, router_rows = rest_rows[0], rest_rows[1], rest_rows[2:]
-        a_here = normed(hidden, gain_one).astype(BF)
-        a_rows = gather_tokens(a_here)
+        if layer_index == 0:
+            a_rows = normed(gather_tokens(inputs).astype(F32), gain_one).astype(BF)
+        else:
+            a_rows = gather_tokens(normed(hidden, gain_one).astype(BF))
         partial_attn, qkv, mixed = attend_ahead(a_rows, w_attn, heads_dim)
         middle = hidden + scatter_tokens(partial_attn)
         b_here = normed(middle, gain_two).astype(BF)
@@ -569,9 +575,13 @@
         (b_here, probs, gate, combined, buffer, pre) = saved[layer_index][8:]
         dc_rows = gather_tokens((gate[:, None] * upstream).astype(BF))
         d_gate = jnp.sum(upstream * combined, -1)
+        if layer_index < LAYERS - 1:
+            dc_rows, attn_shard = lax.optimization_barrier((dc_rows, attn_shard))
+            layer_grads[layer_index + 1] = (attn_shard, expert_shard)
         d_tokens, grad_experts = experts_behind(
             dc_rows, pos_row, pos_col, buffer, pre, w_experts, experts, capacity
         )
+        expert_shard = lax.psum_scatter(grad_experts, "fsdp", scatter_dimension=0, tiled=True)
         d_logits = d_gate[:, None] * gate[:, None] * (pick - probs)
         d_b_here = scatter_tokens(d_tokens)
         for expert in range(experts):
@@ -583,15 +593,14 @@
         d_middle = d_middle + upstream
         da_rows = gather_tokens(d_middle.astype(BF))
         d_a_rows, grad_attn = attend_behind(da_rows, a_rows, qkv, mixed, w_attn)
+        d_a_rows, expert_shard = lax.optimization_barrier((d_a_rows, expert_shard))
+        attn_shard = lax.psum_scatter(grad_attn, "fsdp", scatter_dimension=0, tiled=True)
         d_before, grad_gain_one = normed_back(before, gain_one, scatter_tokens(d_a_rows))
         upstream = d_before + d_middle
-        layer_grads[layer_index] = (
-            lax.psum_scatter(grad_attn, "fsdp", scatter_dimension=0, tiled=True),
-            lax.psum_scatter(grad_experts, "fsdp", scatter_dimension=0, tiled=True),
-        )
         small_sums[layer_index] = jnp.concatenate(
             [grad_gain_one[None], grad_gain_two[None], grad_router], 0
         )
+    layer_grads[0] = (attn_shard, expert_shard)
     sums = lax.psum(jnp.concatenate(small_sums, 0), ("fsdp", "tp"))
     sums = lax.dynamic_slice_in_dim(sums, fsdp_index * shard, shard, 1)
     sums = sums.reshape(LAYERS, 2 + experts, shard)

time: 1180 us -> 782 us (0.66)
  Pallas kernels: 954 us -> 531 us
  waiting for transfers between devices: 83.8 us -> 108 us
  blocking collectives: 54 us -> 40.8 us
    pallas_call x8, Pallas kernels: 556 us -> 198 us  [scatter_tokens(): pl.pallas_call(functools.partial(scatter_body, count), in_specs=[pl.Block...]
    pallas_call x8, Pallas kernels: 275 us -> 211 us  [gather_tokens(): pl.pallas_call(functools.partial(gather_body, count), in_specs=[pl.BlockS...]
    reduce_scatter x2, waiting for transfers between devices: 0.01 us -> 31.1 us  [local(): lax.psum_scatter(grad_attn, 'fsdp', scatter_dimension=0, tiled=True)]
    all_gather x2, waiting for transfers between devices: 17.4 us -> 0.04 us  [local(): lax.all_gather(jnp.concatenate(small, 1), 'fsdp', axis=0, tiled=True)]
    psum x1, blocking collectives: 54 us -> 40.8 us  [local(): sums = lax.psum(jnp.concatenate(small_sums, 0), ('fsdp', 'tp'))]
    unnamed x132 -> x206, local copies, waits for them, and re-layouts: 18.7 us -> 24.6 us
  transfers between devices with their start and end apart: 8 -> 8, of which waited for: 2 -> 2; matrix products, arithmetic and copies ran while one was open for 3% -> 5% of each run, Pallas kernels for 53% -> 44%
where the time goes in v3:
time: 782 us; the launch traced here: 773 us
  Pallas kernels  531 us (68%)
  waiting for transfers between devices  108 us (14%)
  local copies, waits for them, and re-layouts  50.5 us (6%)
  blocking collectives  40.8 us (5%)
  other arithmetic  25.5 us (3%)
  between operations  16 us (2%)
    pallas_call x8, Pallas kernels, gather_tokens(): pl.pallas_call(functools.partial(gather_body, count), in_specs=[pl.BlockS...  211 us
    pallas_call x8, Pallas kernels, scatter_tokens(): pl.pallas_call(functools.partial(scatter_body, count), in_specs=[pl.Block...  198 us
    reduce_scatter x2, waiting for transfers between devices, local(): lax.psum_scatter(grad_experts, 'fsdp', scatter_dimension=0, tiled=True)  76 us
    pallas_call x2, Pallas kernels, attend_behind(): pl.pallas_call(attend_behind_body, grid=(tokens // BLOCK,), in_specs=[who...  45 us
    psum x1, blocking collectives, local(): sums = lax.psum(jnp.concatenate(small_sums, 0), ('fsdp', 'tp'))  40.8 us
    reduce_scatter x2, waiting for transfers between devices, local(): lax.psum_scatter(grad_attn, 'fsdp', scatter_dimension=0, tiled=True)  31.1 us
    pallas_call x2, Pallas kernels, experts_behind(): pl.pallas_call(experts_behind_body, grid=(experts,), in_specs=[whole_spec...  30.3 us
    unnamed x206, local copies, waits for them, and re-layouts  24.6 us
  transfers between devices with their start and end apart: 8, of which 2 were waited for; matrix products, arithmetic and copies ran while one was open for 5% of the time, Pallas kernels for 44%

profile of v3, /device:TPU:0, one launch (start us, length us, event | category | flops | bytes accessed | tf_op | source)
XLA Modules:
  0.0 772.8 jit_solution(14806984398520652732)
XLA Ops:
  16.5 1.7 reshape.153
  19.6 1.7 reshape.155
  21.7 30.9 %shard_map.178 = bf16[1024,768]{1,0:T(8,128)(2,1)} custom-call(bf16[256,768]{1,0:T(8,128)(2,1)} %part_ref.1), custom_call_target="tpu_custom_call" | custom-call | bytes 83886080 | tf_op jit(solution)/shard_map/pallas_call | solution.py:391
  52.6 1.8 fusion
  55.4 1.6 slice_reduce_fusion.3
  57.0 3.1 fusion.2.a_ref
  60.1 12.3 %shard_map.179 = (bf16[1024,768]{1,0:T(8,128)(2,1)S(1)}, bf16[1024,576]{1,0:T(8,128)(2,1)S(1)}, bf16[1024,192]{1,0:T(8,128)(2,1)S(1)}) custom-call(bf16[1024,768]{1,0:T(8,128)(2,1)} %fusion.2.a_ref, bf16[768,896]{1,0:T(8,128)(2,1)S(1)} %copy-done.9), custom_call_target="tpu_custom_call" | custom-call | flops 4429185024 | bytes 8388608 | tf_op jit(solution)/shard_map/pallas_call | solution.py:78
  73.5 24.8 %shard_map.180 = f32[256,768]{1,0:T(8,128)S(1)} custom-call(bf16[1024,768]{1,0:T(8,128)(2,1)S(1)} %get-tuple-element.35.whole_ref), custom_call_target="tpu_custom_call" | custom-call | bytes 83886080 | tf_op jit(solution)/shard_map/pallas_call | solution.py:475
  101.0 28.9 %shard_map.181.b_ref = bf16[1024,768]{1,0:T(8,128)(2,1)} custom-call(bf16[256,768]{1,0:T(8,128)(2,1)} %multiply_convert_fusion.3.part_ref), custom_call_target="tpu_custom_call" | custom-call | bytes 83886080 | tf_op jit(solution)/shard_map/pallas_call | solution.py:391
  131.4 1.6 slice_reduce_fusion.7
  133.6 11.3 %shard_map.182 = (bf16[1024,768]{1,0:T(8,128)(2,1)S(1)}, bf16[1024,768]{1,0:T(8,128)(2,1)S(1)}, f32[1024,768]{1,0:T(8,128)}) custom-call(bf16[1024,768]{1,0:T(8,128)(2,1)S(1)} %copy-done.2, s32[1,1024]{1,0:T(1,128)S(1)} %bitcast.86, s32[1024,1]{1,0:T(8,128)S(1)} %copy.43.col_ref, bf16[768,6144]{1,0:T(8,128)(2,1)} %all-gather.7.cloned.1.call-done.w_ref), custom_call_target="tpu_custom_call" | custom-call | flops 5637144576 | bytes 20971520 | tf_op jit(solution)/shard_map/pallas_call | solution.py:207
  144.9 24.6 %shard_map.183 = f32[256,768]{1,0:T(8,128)S(1)} custom-call(bf16[1024,768]{1,0:T(8,128)(2,1)S(1)} %get-tuple-element.36.whole_ref), custom_call_target="tpu_custom_call" | custom-call | bytes 83886080 | tf_op jit(solution)/shard_map/pallas_call | solution.py:475
  171.5 26.6 %shard_map.184.a_ref = bf16[1024,768]{1,0:T(8,128)(2,1)} custom-call(bf16[256,768]{1,0:T(8,128)(2,1)} %multiply_convert_fusion.2.part_ref), custom_call_target="tpu_custom_call" | custom-call | bytes 83886080 | tf_op jit(solution)/shard_map/pallas_call | solution.py:391
  198.2 12.2 %shard_map.185 = (bf16[1024,768]{1,0:T(8,128)(2,1)S(1)}, bf16[1024,576]{1,0:T(8,128)(2,1)S(1)}, bf16[1024,192]{1,0:T(8,128)(2,1)S(1)}) custom-call(bf16[1024,768]{1,0:T(8,128)(2,1)} %shard_map.184.a_ref, bf16[768,896]{1,0:T(8,128)(2,1)S(1)} %copy-done.11), custom_call_target="tpu_custom_call" | custom-call | flops 4429185024 | bytes 8388608 | tf_op jit(solution)/shard_map/pallas_call | solution.py:78
  211.5 24.5 %shard_map.186 = f32[256,768]{1,0:T(8,128)S(1)} custom-call(bf16[1024,768]{1,0:T(8,128)(2,1)S(1)} %get-tuple-element.37.whole_ref), custom_call_target="tpu_custom_call" | custom-call | bytes 83886080 | tf_op jit(solution)/shard_map/pallas_call | solution.py:475
  238.0 24.3 %shard_map.187.b_ref = bf16[1024,768]{1,0:T(8,128)(2,1)} custom-call(bf16[256,768]{1,0:T(8,128)(2,1)} %multiply_convert_fusion.1.part_ref), custom_call_target="tpu_custom_call" | custom-call | bytes 83886080 | tf_op jit(solution)/shard_map/pallas_call | solution.py:391
  263.4 1.4 copy-done.4
  264.8 11.0 %shard_map.188 = (bf16[1024,768]{1,0:T(8,128)(2,1)S(1)}, bf16[1024,768]{1,0:T(8,128)(2,1)S(1)}, f32[1024,768]{1,0:T(8,128)}) custom-call(bf16[1024,768]{1,0:T(8,128)(2,1)S(1)} %copy-done.4, s32[1,1024]{1,0:T(1,128)S(1)} %bitcast.87, s32[1024,1]{1,0:T(8,128)S(1)} %copy.43.col_ref, bf16[768,6144]{1,0:T(8,128)(2,1)} %all-gather.11.cloned.1.call-done.w_ref), custom_call_target="tpu_custom_call" | custom-call | flops 5637144576 | bytes 20971520 | tf_op jit(solution)/shard_map/pallas_call | solution.py:207
  275.8 24.7 %shard_map.189 = f32[256,768]{1,0:T(8,128)S(1)} custom-call(bf16[1024,768]{1,0:T(8,128)(2,1)S(1)} %get-tuple-element.38.whole_ref), custom_call_target="tpu_custom_call" | custom-call | bytes 83886080 | tf_op jit(solution)/shard_map/pallas_call | solution.py:475
  301.5 22.8 %shard_map.190.dc_ref = bf16[1024,768]{1,0:T(8,128)(2,1)} custom-call(bf16[256,768]{1,0:T(8,128)(2,1)} %get-tuple-element.122.part_ref), custom_call_target="tpu_custom_call" | custom-call | bytes 83886080 | tf_op jit(solution)/shard_map/pallas_call | solution.py:391
  324.3 1.4 copy-done.5
  325.7 1.4 copy-done.16
  327.1 15.1 %shard_map.191 = (bf16[1024,768]{1,0:T(8,128)(2,1)S(1)}, bf16[768,6144]{1,0:T(8,128)(2,1)}) custom-call(bf16[1024,768]{1,0:T(8,128)(2,1)S(1)} %copy-done.5, s32[1,1024]{1,0:T(1,128)S(1)} %bitcast.88, s32[1024,1]{1,0:T(8,128)S(1)} %copy.43.col_ref, bf16[1024,768]{1,0:T(8,128)(2,1)S(1)} %copy-done.16, f32[1024,768]{1,0:T(8,128)} %get-tuple-element.40.pre_ref, ...), custom_call_target="tpu_custom_call" | custom-call | flops 8053063680 | bytes 31457280 | tf_op jit(solution)/shard_map/pallas_call | solution.py:265
  343.5 1.5 copy-done.1
  345.0 21.8 %shard_map.192 = f32[256,768]{1,0:T(8,128)S(1)} custom-call(bf16[1024,768]{1,0:T(8,128)(2,1)S(1)} %copy-done.1), custom_call_target="tpu_custom_call" | custom-call | bytes 83886080 | tf_op jit(solution)/shard_map/pallas_call | solution.py:475
  368.2 1.9 multiply_reduce_fusion
  370.1 1.6 fusion.26
  371.7 20.8 %shard_map.193.da_ref = bf16[1024,768]{1,0:T(8,128)(2,1)} custom-call(bf16[256,768]{1,0:T(8,128)(2,1)} %get-tuple-element.119.part_ref), custom_call_target="tpu_custom_call" | custom-call | bytes 83886080 | tf_op jit(solution)/shard_map/pallas_call | solution.py:391
  392.6 1.4 copy-done.12
  394.0 1.3 copy-done.20
  396.3 22.0 %shard_map.194 = (bf16[1024,768]{1,0:T(8,128)(2,1)S(1)}, bf16[768,768]{1,0:T(8,128)(2,1)S(1)}) custom-call(bf16[1024,768]{1,0:T(8,128)(2,1)} %shard_map.193.da_ref, bf16[1024,768]{1,0:T(8,128)(2,1)} %shard_map.184.a_ref, bf16[1024,576]{1,0:T(8,128)(2,1)S(1)} %copy-done.20, bf16[1024,192]{1,0:T(8,128)(2,1)S(1)} %copy-done.24, bf16[768,896]{1,0:T(8,128)(2,1)S(1)} %copy-done.12), custom_call_target="tpu_custom_call" | custom-call | flops 10468982784 | bytes 10485760 | tf_op jit(solution)/shard_map/pallas_call | solution.py:148
  419.6 25.9 %shard_map.195 = f32[256,768]{1,0:T(8,128)S(1)} custom-call(bf16[1024,768]{1,0:T(8,128)(2,1)S(1)} %get-tuple-element.46.whole_ref), custom_call_target="tpu_custom_call" | custom-call | bytes 83886080 | tf_op jit(solution)/shard_map/pallas_call | solution.py:475
  446.5 1.5 multiply_convert_fusion
  448.9 29.7 %shard_map.196.dc_ref = bf16[1024,768]{1,0:T(8,128)(2,1)} custom-call(bf16[256,768]{1,0:T(8,128)(2,1)} %get-tuple-element.101.part_ref), custom_call_target="tpu_custom_call" | custom-call | bytes 83886080 | tf_op jit(solution)/shard_map/pallas_call | solution.py:391
  478.8 1.4 copy-done.3
  480.2 15.1 %shard_map.197 = (bf16[1024,768]{1,0:T(8,128)(2,1)S(1)}, bf16[768,6144]{1,0:T(8,128)(2,1)}) custom-call(bf16[1024,768]{1,0:T(8,128)(2,1)S(1)} %copy-done.3, s32[1,1024]{1,0:T(1,128)S(1)} %bitcast.89, s32[1024,1]{1,0:T(8,128)S(1)} %copy-done.8, bf16[1024,768]{1,0:T(8,128)(2,1)S(1)} %copy-done.14, f32[1024,768]{1,0:T(8,128)} %get-tuple-element.50.pre_ref, ...), custom_call_target="tpu_custom_call" | custom-call | flops 8053063680 | bytes 31457280 | tf_op jit(solution)/shard_map/pallas_call | solution.py:265
  495.4 24.6 %shard_map.198 = f32[256,768]{1,0:T(8,128)S(1)} custom-call(bf16[1024,768]{1,0:T(8,128)(2,1)S(1)} %get-tuple-element.51.whole_ref), custom_call_target="tpu_custom_call" | custom-call | bytes 83886080 | tf_op jit(solution)/shard_map/pallas_call | solution.py:475
  520.7 1.5 fusion.27
  522.2 26.6 %shard_map.199.da_ref = bf16[1024,768]{1,0:T(8,128)(2,1)} custom-call(bf16[256,768]{1,0:T(8,128)(2,1)} %get-tuple-element.99.part_ref), custom_call_target="tpu_custom_call" | custom-call | bytes 83886080 | tf_op jit(solution)/shard_map/pallas_call | solution.py:391
  548.8 1.3 copy-done.18
  550.1 23.0 %shard_map.200 = (bf16[1024,768]{1,0:T(8,128)(2,1)S(1)}, bf16[768,768]{1,0:T(8,128)(2,1)}) custom-call(bf16[1024,768]{1,0:T(8,128)(2,1)} %shard_map.199.da_ref, bf16[1024,768]{1,0:T(8,128)(2,1)} %fusion.2.a_ref, bf16[1024,576]{1,0:T(8,128)(2,1)S(1)} %copy-done.18, bf16[1024,192]{1,0:T(8,128)(2,1)S(1)} %copy-done.22, bf16[768,896]{1,0:T(8,128)(2,1)S(1)} %copy-done.10), custom_call_target="tpu_custom_call" | custom-call | flops 10468982784 | bytes 10485760 | tf_op jit(solution)/shard_map/pallas_call | solution.py:148
  574.4 2.0 stack.38
  577.9 31.0 %reduce-scatter.11.cloned.1.call-done = bf16[96,768]{1,0:T(8,128)(2,1)} async-done(((bf16[768,768]{1,0:T(8,128)(2,1)}), bf16[96,768]{1,0:T(8,128)(2,1)}) %reduce-scatter.11.cloned.1.call-update) | async-done | bytes 147472 | tf_op jit(solution)/shard_map/reduce_scatter | solution.py:597
  613.0 76.0 %reduce-scatter.9.cloned.1.call-done = bf16[96,6144]{1,0:T(8,128)(2,1)} async-done(((bf16[768,6144]{1,0:T(8,128)(2,1)}), bf16[96,6144]{1,0:T(8,128)(2,1)}) %reduce-scatter.9.cloned.1.call-update) | async-done | bytes 1179664 | tf_op jit(solution)/shard_map/reduce_scatter | solution.py:584
  689.0 27.0 %shard_map.201 = f32[256,768]{1,0:T(8,128)S(1)} custom-call(bf16[1024,768]{1,0:T(8,128)(2,1)S(1)} %get-tuple-element.56.whole_ref), custom_call_target="tpu_custom_call" | custom-call | bytes 83886080 | tf_op jit(solution)/shard_map/pallas_call | solution.py:475
  716.3 40.8 %psum.7 = f32[12,768]{1,0:T(8,128)S(1)} all-reduce(f32[12,768]{1,0:T(8,128)S(1)} %concatenate.12), channel_id=1, replica_groups=mesh['fsdp'=8,'tp'=4] {'fsdp','tp'}, use_global_device_ids=true, to_apply=%region_25.26 | all-reduce | flops 9216 | bytes 73728 | tf_op jit(solution)/shard_map/psum | solution.py:604
  758.3 2.0 stack.37
  761.9 2.6 slice_bitcast_fusion
  (297 shorter events, 42.9 us)
Async XLA Ops:
  7.2 47.3 %all-gather.5.cloned.1.call-start = ((), (), s32[]{:S(2)}) async-start(), calls=%async_computation.4 | async-start | bytes 1548288 | tf_op jit(solution)/shard_map/all_gather | solution.py:533
  13.0 117.4 %all-gather.9.cloned.1.call-start = ((), (), s32[]{:S(2)}) async-start(), calls=%async_computation.6 | async-start | bytes 1548288 | tf_op jit(solution)/shard_map/all_gather | solution.py:533
  14.6 119.0 %all-gather.7.cloned.1.call-start = ((), (), s32[]{:S(2)}) async-start(), calls=%async_computation.5 | async-start | bytes 10616832 | tf_op jit(solution)/shard_map/all_gather | solution.py:534
  18.3 245.1 %all-gather.11.cloned.1.call-start = ((), (), s32[]{:S(2)}) async-start(), calls=%async_computation.7 | async-start | bytes 10616832 | tf_op jit(solution)/shard_map/all_gather | solution.py:534
  21.3 398.1 %reduce-scatter.5.cloned.1.call-start = ((), (), s32[]{:S(2)}) async-start(), calls=%async_computation.8 | async-start | bytes 10616832 | tf_op jit(solution)/shard_map/reduce_scatter | solution.py:584
  21.5 241.3 %copy-start.64 = (s32[256]{0:T(256)}, s32[256]{0:T(256)S(1)}, u32[]{:S(2)}) copy-start(s32[256]{0:T(256)S(1)} %dynamic_slice.6) | copy-start | bytes 3076
  21.7 302.6 %copy-start.7 = (s32[1024,1]{1,0:T(8,128)}, s32[1024,1]{1,0:T(8,128)S(1)}, u32[]{:S(2)}) copy-start(s32[1024,1]{1,0:T(8,128)S(1)} %copy.43.col_ref) | copy-start | bytes 12292
  73.5 25.7 %copy-start.21 = (bf16[1024,192]{1,0:T(8,128)(2,1)}, bf16[1024,192]{1,0:T(8,128)(2,1)S(1)}, u32[]{:S(2)}) copy-start(bf16[1024,192]{1,0:T(8,128)(2,1)S(1)} %get-tuple-element.53.mixed_ref) | copy-start | bytes 1179652
  99.2 30.7 %copy-start.90 = (f32[256]{0:T(256)}, f32[256]{0:T(256)S(1)}, u32[]{:S(2)}) copy-start(f32[256]{0:T(256)S(1)} %get-tuple-element.111) | copy-start | bytes 3076
  99.2 30.7 %copy-start.73 = (f32[256]{0:T(256)}, f32[256]{0:T(256)S(1)}, u32[]{:S(2)}) copy-start(f32[256]{0:T(256)S(1)} %fusion.22) | copy-start | bytes 3076
  100.9 28.9 %copy-start.38 = (bf16[256,768]{1,0:T(8,128)(2,1)S(1)}, bf16[256,768]{1,0:T(8,128)(2,1)}, u32[]{:S(2)}) copy-start(bf16[256,768]{1,0:T(8,128)(2,1)} %multiply_convert_fusion.3.part_ref) | copy-start | bytes 1179652
  133.0 36.8 %copy-start.48 = (f32[768]{0:T(1024)}, f32[768]{0:T(1024)S(1)}, u32[]{:S(2)}) copy-start(f32[768]{0:T(1024)S(1)} %get-tuple-element.98) | copy-start | bytes 9220
  133.6 35.9 %copy-start.75 = (f32[256]{0:T(256)}, f32[256]{0:T(256)S(1)}, u32[]{:S(2)}) copy-start(f32[256]{0:T(256)S(1)} %get-tuple-element.109) | copy-start | bytes 3076
  169.8 28.4 %copy-start.92 = (f32[256]{0:T(256)}, f32[256]{0:T(256)S(1)}, u32[]{:S(2)}) copy-start(f32[256]{0:T(256)S(1)} %get-tuple-element.107) | copy-start | bytes 3076
  169.8 28.3 %copy-start.79 = (f32[256]{0:T(256)}, f32[256]{0:T(256)S(1)}, u32[]{:S(2)}) copy-start(f32[256]{0:T(256)S(1)} %fusion.23) | copy-start | bytes 3076
  170.7 27.5 %copy-start.11 = (bf16[768,896]{1,0:T(8,128)(2,1)S(1)}, bf16[768,896]{1,0:T(8,128)(2,1)}, u32[]{:S(2)}) copy-start(bf16[768,896]{1,0:T(8,128)(2,1)} %all-gather.9.cloned.1.call-done.w_ref) | copy-start | bytes 4128772
  263.4 80.1 %copy-start.77 = (f32[256]{0:T(256)}, f32[256]{0:T(256)S(1)}, u32[]{:S(2)}) copy-start(f32[256]{0:T(256)S(1)} %get-tuple-element.103) | copy-start | bytes 3076
  275.8 25.6 %copy-start.15 = (bf16[1024,768]{1,0:T(8,128)(2,1)}, bf16[1024,768]{1,0:T(8,128)(2,1)S(1)}, u32[]{:S(2)}) copy-start(bf16[1024,768]{1,0:T(8,128)(2,1)S(1)} %get-tuple-element.39.buffer_ref) | copy-start | bytes 4718596
  343.4 135.3 %reduce-scatter.7.cloned.1.call-start = ((), (), s32[]{:S(2)}) async-start(), calls=%async_computation.9 | async-start | bytes 1327104 | tf_op jit(solution)/shard_map/reduce_scatter | solution.py:597
  345.0 25.1 %copy-start.78 = (f32[256]{0:T(256)S(1)}, f32[256]{0:T(256)}, u32[]{:S(2)}) copy-start(f32[256]{0:T(256)} %copy-done.77) | copy-start | bytes 3076
  419.3 189.6 %reduce-scatter.11.cloned.1.call-start = ((), (), s32[]{:S(2)}) async-start(), calls=%async_computation.11 | async-start | bytes 1327104 | tf_op jit(solution)/shard_map/reduce_scatter | solution.py:597
  419.4 26.1 %copy-start.30 = (f32[256,768]{1,0:T(8,128)S(1)}, f32[256,768]{1,0:T(8,128)}, u32[]{:S(2)}) copy-start(f32[256,768]{1,0:T(8,128)} %copy-done.28) | copy-start | bytes 2359300
  419.4 26.1 %copy-start.49 = (f32[768]{0:T(1024)S(1)}, f32[768]{0:T(1024)}, u32[]{:S(2)}) copy-start(f32[768]{0:T(1024)} %copy-done.48) | copy-start | bytes 9220
  419.4 26.1 %copy-start.80 = (f32[256]{0:T(256)S(1)}, f32[256]{0:T(256)}, u32[]{:S(2)}) copy-start(f32[256]{0:T(256)} %copy-done.79) | copy-start | bytes 3076
  419.5 26.9 %copy-start.93 = (f32[256]{0:T(256)S(1)}, f32[256]{0:T(256)}, u32[]{:S(2)}) copy-start(f32[256]{0:T(256)} %copy-done.92) | copy-start | bytes 3076
  419.5 26.9 %copy-start.33 = (f32[256,768]{1,0:T(8,128)S(1)}, f32[256,768]{1,0:T(8,128)}, u32[]{:S(2)}) copy-start(f32[256,768]{1,0:T(8,128)} %copy-done.31) | copy-start | bytes 2359300
  419.5 26.9 %copy-start.51 = (f32[768]{0:T(1024)S(1)}, f32[768]{0:T(1024)}, u32[]{:S(2)}) copy-start(f32[768]{0:T(1024)} %get-tuple-element.93) | copy-start | bytes 9220
  419.5 26.9 %copy-start.53 = (f32[768]{0:T(1024)S(1)}, f32[768]{0:T(1024)}, u32[]{:S(2)}) copy-start(f32[768]{0:T(1024)} %get-tuple-element.94) | copy-start | bytes 9220
  419.5 26.9 %copy-start.55 = (f32[768]{0:T(1024)S(1)}, f32[768]{0:T(1024)}, u32[]{:S(2)}) copy-start(f32[768]{0:T(1024)} %get-tuple-element.95) | copy-start | bytes 9220
  419.5 26.9 %copy-start.57 = (f32[768]{0:T(1024)S(1)}, f32[768]{0:T(1024)}, u32[]{:S(2)}) copy-start(f32[768]{0:T(1024)} %get-tuple-element.96) | copy-start | bytes 9220
  419.5 26.9 %copy-start.69 = (f32[256]{0:T(256)S(1)}, f32[256]{0:T(256)}, u32[]{:S(2)}) copy-start(f32[256]{0:T(256)} %copy-done.67) | copy-start | bytes 3076
  419.5 26.9 %copy-start.76 = (f32[256]{0:T(256)S(1)}, f32[256]{0:T(256)}, u32[]{:S(2)}) copy-start(f32[256]{0:T(256)} %copy-done.75) | copy-start | bytes 3076
  419.5 26.9 %copy-start.82 = (f32[256,1]{0,1:T(1,128)S(1)}, f32[256,1]{0,1:T(1,128)}, u32[]{:S(2)}) copy-start(f32[256,1]{0,1:T(1,128)} %copy-done.81) | copy-start | bytes 3076
  419.5 26.9 %copy-start.84 = (f32[256,1]{0,1:T(1,128)S(1)}, f32[256,1]{0,1:T(1,128)}, u32[]{:S(2)}) copy-start(f32[256,1]{0,1:T(1,128)} %copy-done.83) | copy-start | bytes 3076
  419.6 26.9 %copy-start.86 = (f32[256,1]{0,1:T(1,128)S(1)}, f32[256,1]{0,1:T(1,128)}, u32[]{:S(2)}) copy-start(f32[256,1]{0,1:T(1,128)} %copy-done.85) | copy-start | bytes 3076
  419.6 26.9 %copy-start.88 = (f32[256,1]{0,1:T(1,128)S(1)}, f32[256,1]{0,1:T(1,128)}, u32[]{:S(2)}) copy-start(f32[256,1]{0,1:T(1,128)} %copy-done.87) | copy-start | bytes 3076
  419.6 26.9 %copy-start.97 = (f32[256]{0:T(256)S(1)}, f32[256]{0:T(256)}, u32[]{:S(2)}) copy-start(f32[256]{0:T(256)} %copy-done.96) | copy-start | bytes 3076
  448.0 30.7 %copy-start.66 = (s32[256]{0:T(256)S(1)}, s32[256]{0:T(256)}, u32[]{:S(2)}) copy-start(s32[256]{0:T(256)} %copy-done.64) | copy-start | bytes 3076
  448.0 30.7 %copy-start.72 = (f32[256,4]{0,1:T(4,128)S(1)}, f32[256,4]{0,1:T(4,128)}, u32[]{:S(2)}) copy-start(f32[256,4]{0,1:T(4,128)} %get-tuple-element.110) | copy-start | bytes 12292
  448.0 30.7 %copy-start.8 = (s32[1024,1]{1,0:T(8,128)S(1)}, s32[1024,1]{1,0:T(8,128)}, u32[]{:S(2)}) copy-start(s32[1024,1]{1,0:T(8,128)} %copy-done.7) | copy-start | bytes 12292
  448.0 30.8 %copy-start.14 = (bf16[1024,768]{1,0:T(8,128)(2,1)S(1)}, bf16[1024,768]{1,0:T(8,128)(2,1)}, u32[]{:S(2)}) copy-start(bf16[1024,768]{1,0:T(8,128)(2,1)} %copy-done.13) | copy-start | bytes 4718596
  495.4 25.3 %copy-start.91 = (f32[256]{0:T(256)S(1)}, f32[256]{0:T(256)}, u32[]{:S(2)}) copy-start(f32[256]{0:T(256)} %copy-done.90) | copy-start | bytes 3076
  495.4 25.3 %copy-start.35 = (f32[256,768]{1,0:T(8,128)S(1)}, f32[256,768]{1,0:T(8,128)}, u32[]{:S(2)}) copy-start(f32[256,768]{1,0:T(8,128)} %copy-done.34) | copy-start | bytes 2359300
  522.2 26.6 %copy-start.10 = (bf16[768,896]{1,0:T(8,128)(2,1)S(1)}, bf16[768,896]{1,0:T(8,128)(2,1)}, u32[]{:S(2)}) copy-start(bf16[768,896]{1,0:T(8,128)(2,1)} %all-gather.5.cloned.1.call-done.w_ref) | copy-start | bytes 4128772
  522.2 26.6 %copy-start.22 = (bf16[1024,192]{1,0:T(8,128)(2,1)S(1)}, bf16[1024,192]{1,0:T(8,128)(2,1)}, u32[]{:S(2)}) copy-start(bf16[1024,192]{1,0:T(8,128)(2,1)} %copy-done.21) | copy-start | bytes 1179652
  573.1 115.9 %reduce-scatter.9.cloned.1.call-start = ((), (), s32[]{:S(2)}) async-start(), calls=%async_computation.10 | async-start | bytes 10616832 | tf_op jit(solution)/shard_map/reduce_scatter | solution.py:584
  576.4 32.6 %copy-start.47 = (bf16[96,768]{1,0:T(8,128)(2,1)S(1)}, bf16[96,768]{1,0:T(8,128)(2,1)}, u32[]{:S(2)}) copy-start(bf16[96,768]{1,0:T(8,128)(2,1)} %reduce-scatter.7.cloned.1.call-done) | copy-start | bytes 442372
  611.9 104.1 %copy-start.37 = (bf16[256,768]{1,0:T(8,128)(2,1)S(1)}, bf16[256,768]{1,0:T(8,128)(2,1)}, u32[]{:S(2)}) copy-start(bf16[256,768]{1,0:T(8,128)(2,1)} %part_ref.1) | copy-start | bytes 1179652
  (60 other events, 582.2 us)
Sparse Core Ops, SparseCore 0:
  13.1 27.5 all-gather.4
  43.2 24.8 all-gather.8
  70.5 58.8 all-gather.6
  131.1 58.8 all-gather.10
  343.5 74.7 reduce-scatter.4
  422.0 36.7 reduce-scatter.6
  573.2 35.7 reduce-scatter.10
  612.5 76.4 reduce-scatter.8
